TPU v7x, 32 devices: a whole 2x2x4 slice. The times are simulated.
32 devices in a mesh: space: 16 (over z, y, core), dp: 2 (over x).
Axes of the slice: x: 2, y: 2, z: 4, core: 2. Of those that a mesh axis runs over, the one named last changes fastest.
Arguments:
- node_features: float32 [2, 128, 4096], P('dp', None, 'space'), may hold values from -6 to 6
- positions: float32 [2, 3, 4096], P('dp', None, 'space')
- species: int32 [2, 4096], P('dp', 'space'), may hold values from 0 to 7
- energy_cotangent: float32 [2, 4096], P('dp', 'space'), may hold values from -6 to 6
- pair_target: int32 [2, 320], P('dp', 'space'), may hold values from 0 to 3, as said below
- pair_source: int32 [2, 320], P('dp', 'space'), may hold values from 0 to 7, as said below
- pair_count: int32 [2, 16], P('dp', 'space'), may hold values from 4 to 20, as said below
- radial_weight: float32 [8, 128], replicated, may hold values from -2 to 2
- mix_weight: bfloat16 [384, 128], replicated, may hold values from -0.3125 to 0.3125
- readout_weight: float32 [128], replicated, may hold values from -0.5 to 0.5
- species_shift: float32 [8], replicated, may hold values from -4 to 4
Outputs:
- atom_energy: float32 [2, 4096], P('dp', 'space')
- feature_grad: float32 [2, 128, 4096], P('dp', None, 'space')
- radial_grad: float32 [8, 128], replicated
- mix_grad: float32 [384, 128], replicated
- readout_grad: float32 [128], replicated
- shift_grad: float32 [8], replicated
Inputs may be any that keep to these rules, and one draw needn't show every extreme that they name: `pair_target`: the target cell of a slot lies in its slab. `pair_source`: A live slot's source cell lies within 2 cells of its target cell and inside the snapshot; every target cell pairs with itself; no pair appears twice in a slab. `pair_count`: counts differ from slab to slab; in every snapshot some slab uses all 20 slots.
All inputs are finite; a program needn't handle non-finite values.
Results may differ from a plain program's by a relative error of at most 0.0009.
The roundings to bfloat16 on the way count: a program that leaves them out, or rounds other values in their place, can miss the bound.
Values sent between devices are 32-bit elements; how exact they have to be, the bound alone decides.
No kernel may reach another device: no remote copies, remote signals or barrier semaphores. Data moves between devices by JAX's collectives and lax.ppermute only.
A program may use at most 64 MiB of HBM per device.

v0:
```python
import functools
import math

import jax
import jax.numpy as jnp
from jax import lax
from jax.experimental import pallas as pl
from jax.experimental.pallas import tpu as pltpu
from jax.sharding import PartitionSpec as P

CH = 128
NB = 8
NY = 9
NSPEC = 8
CELL_ATOMS = 64
HALO_CELLS = 2
GROUP = 2 * CELL_ATOMS
ROWS = 16
WIDTH = 256
CHUNKS = -(-NY * GROUP // WIDTH)

cutoff = 5.0
message_scale = 0.25

COS_COEFFS = (
    0.9999999998846169,
    -4.934802185771876,
    4.058711815779763,
    -1.3352602773967561,
    0.23532080049888648,
    -0.025785772074137014,
    0.0019043022864480008,
    -8.868331860867329e-05,
)
SINC_COEFFS = (
    0.9999999992502204,
    -1.6449339933418936,
    0.8117412468909989,
    -0.1907447263221115,
    0.02612742969685046,
    -0.0023157632409761065,
    0.00012580778956459784,
)

MIX_ROWS = 3 * CH
HALF = MIX_ROWS // 2
QUARTER = MIX_ROWS // 4
REST = 16
CELLS = 4 + 2 * HALO_CELLS
SMALL = 3
LATER = 5
SLAB_ROWS = CH + 8


def polynomial(coeffs, x):
    total = coeffs[-1] * x + coeffs[-2]
    for c in coeffs[-3::-1]:
        total = total * x + c
    return total


def factor_rows(factor_ref, size, row, source, target, keep):
    dx = (target[0] - source[0]) * (1.0 / cutoff)
    dy = (target[1] - source[1]) * (1.0 / cutoff)
    dz = (target[2] - source[2]) * (1.0 / cutoff)
    xx, yy, zz = dx * dx, dy * dy, dz * dz
    square = xx + yy + zz
    inside = jnp.minimum(square, 1.0)
    gap = 1.0 - inside
    base = (gap * gap) * keep * polynomial(SINC_COEFFS, inside)
    twice_cos = polynomial([2.0 * c for c in COS_COEFFS], inside)
    raw = [base, twice_cos * base]
    for _ in range(NB - 2):
        raw.append(twice_cos * raw[-1] - raw[-2])
    radial = [value if b == 0 else value * (1.0 / (b + 1)) for b, value in enumerate(raw)]
    root_three = math.sqrt(3.0)
    root_fifteen = math.sqrt(15.0)
    root_five = math.sqrt(5.0)
    wide_x = root_fifteen * dx
    harmonic = [
        None,
        root_three * dx,
        root_three * dy,
        root_three * dz,
        wide_x * dy,
        (root_fifteen * dy) * dz,
        (0.5 * root_five) * (3.0 * zz - square),
        wide_x * dz,
        (0.5 * root_fifteen) * (xx - yy),
    ]
    for b in range(NB):
        rows = slice(b * size + row, b * size + row + ROWS)
        for y in range(NY):
            value = radial[b] if y == 0 else radial[b] * harmonic[y]
            factor_ref[rows, y * GROUP : (y + 1) * GROUP] = value.astype(jnp.bfloat16)


def column_to_row(column, size):
    wide = jnp.broadcast_to(column, (size, GROUP))
    at = lax.broadcasted_iota(jnp.int32, (size, GROUP), 0)
    lane = lax.broadcasted_iota(jnp.int32, (size, GROUP), 1)
    return jnp.sum(jnp.where(at == lane, wide, 0.0), axis=0, keepdims=True)


def split_kernel(*refs):
    features_ref, place_in_ref, *inputs = refs[: SMALL + 2]
    near_ref, far_ref, *outputs = refs[SMALL + 2 : 2 * SMALL + 4]
    place_ref, sems = refs[2 * SMALL + 4 :]
    core = lax.axis_index("space") % 2
    place_copy = pltpu.make_async_copy(place_in_ref, place_ref, sems.at[2])
    place_copy.start()
    copies = []
    for k, (ref, side) in enumerate(((near_ref, 1 - core), (far_ref, core))):
        at = pl.ds(pl.multiple_of(side * GROUP, GROUP), GROUP)
        copies.append(
            pltpu.make_async_copy(features_ref.at[0, :, at], ref.at[pl.ds(0, CH)], sems.at[k])
        )
    for k, (src, dst) in enumerate(zip(inputs, outputs)):
        copies.append(pltpu.make_async_copy(src, dst, sems.at[3 + k]))
    for copy in copies:
        copy.start()
    place_copy.wait()
    low, high = slice(GROUP), slice(GROUP, 2 * GROUP)
    filler = jnp.zeros((5, GROUP), jnp.float32)
    for ref, one, two in ((near_ref, high, low), (far_ref, low, high)):
        rows = [
            jnp.where(core == 0, place_ref[axis, :, one], place_ref[axis, :, two]) for axis in range(3)
        ]
        ref[CH:, :] = jnp.concatenate(rows + [filler], axis=0)
    for copy in copies:
        copy.wait()


def live_flags(count, pair_target, pair_source):
    size = (4 * CELLS, pair_target.shape[1])
    at = lax.broadcasted_iota(jnp.int32, size, 0)
    slot = lax.broadcasted_iota(jnp.int32, size, 1)
    hit = (pair_target * CELLS + pair_source == at) & (slot < count)
    return jnp.max(jnp.where(hit, message_scale, 0.0), axis=1, keepdims=True)


def keep_row(flags, t, low, high):
    lane = lax.broadcasted_iota(jnp.int32, (1, GROUP), 1)
    one, two = (2 * t) * CELLS + low, (2 * t + 1) * CELLS + high
    return jnp.where(lane < CELL_ATOMS, flags[one : one + 1], flags[two : two + 1])


def set_group(scaled_ref, features, weight_t):
    for b in range(NB):
        scaled_ref[:, b * GROUP : (b + 1) * GROUP] = (features * weight_t[:, b : b + 1]).astype(
            jnp.bfloat16
        )


def set_cell(scaled_ref, features, half, weight_t):
    first = lax.broadcasted_iota(jnp.int32, (CH, GROUP), 1) < CELL_ATOMS
    turned = pltpu.roll(features, CELL_ATOMS, 1)
    twice = jnp.where(first, features, turned) if half == 0 else jnp.where(first, turned, features)
    for k in range(NB // 2):
        weights = jnp.where(first, weight_t[:, 2 * k : 2 * k + 1], weight_t[:, 2 * k + 1 : 2 * k + 2])
        scaled_ref[:, k * GROUP : (k + 1) * GROUP] = (twice * weights).astype(jnp.bfloat16)


def set_place(place_ref, slab):
    place = slab[CH:].T
    for axis in range(3):
        place_ref[axis] = jnp.broadcast_to(place[:, axis : axis + 1], (GROUP, GROUP))


def fill_steps(factor_ref, size, source_of, keeps, target, diagonal=False):
    def step(row):
        keep = jnp.broadcast_to(keeps[row // CELL_ATOMS], (ROWS, GROUP))
        if diagonal:
            row_at = lax.broadcasted_iota(jnp.int32, (ROWS, GROUP), 0)
            lane_at = lax.broadcasted_iota(jnp.int32, (ROWS, GROUP), 1)
            keep = jnp.where(row_at + row == lane_at, 0.0, keep)
        factor_rows(factor_ref, size, row, source_of(row), target, keep)

    return [functools.partial(step, row) for row in range(0, size, ROWS)]


def rows_of(place_ref, start):
    return lambda row: [place_ref[axis, start + row : start + row + ROWS, :] for axis in range(3)]


def merged_rows(low_ref, low_start, high_ref, high_start):
    low, high = rows_of(low_ref, low_start), rows_of(high_ref, high_start)

    def rows(row):
        first = lax.broadcasted_iota(jnp.int32, (ROWS, GROUP), 1) < CELL_ATOMS
        return [jnp.where(first, one, two) for one, two in zip(low(row), high(row))]

    return rows


def product_steps(scaled_ref, factor_ref, totals, merged=False):
    def step(k):
        width = min(WIDTH, NY * GROUP - k * WIDTH)
        product = jnp.dot(
            scaled_ref[...],
            factor_ref[:, k * WIDTH : k * WIDTH + width],
            preferred_element_type=jnp.float32,
        )
        if merged:
            lane = lax.broadcasted_iota(jnp.int32, (CH, width), 1) % GROUP
            product = jnp.where(lane < CELL_ATOMS, product[:CH], product[CH:])
        totals[k] = product if totals[k] is None else totals[k] + product

    return [functools.partial(step, k) for k in range(CHUNKS)]


def interleave(one, two):
    done = 0
    for k, step in enumerate(one):
        step()
        upto = (k + 1) * len(two) // len(one)
        for other in two[done:upto]:
            other()
        done = upto


def local_kernel(*refs):
    count_ref, pair_target_ref, pair_source_ref, radial_ref, near_ref, far_ref = refs[:6]
    later_in = refs[6 : 6 + LATER]
    group_factor_ref, cell_factor_ref, messages_ref, keep_ref, place_ref = refs[6 + LATER : 11 + LATER]
    later_out = refs[11 + LATER : 11 + 2 * LATER]
    group_ref, cell_ref, sems = refs[11 + 2 * LATER :]
    copies = [
        pltpu.make_async_copy(src, dst, sems.at[k]) for k, (src, dst) in enumerate(zip(later_in, later_out))
    ]
    for copy in copies:
        copy.start()
    even = lax.axis_index("space") % 2 == 0
    near, far = near_ref[...], far_ref[...]
    slabs = (jnp.where(even, far, near), jnp.where(even, near, far))
    targets = [[slab[CH + axis : CH + axis + 1] for axis in range(3)] for slab in slabs]
    flags = live_flags(count_ref[0, 0], pair_target_ref[...], pair_source_ref[...])
    weight_t = radial_ref[...].T
    for g in range(2):
        set_place(place_ref.at[g], slabs[g])
        set_group(group_ref.at[g], slabs[g][:CH], weight_t)
        set_cell(cell_ref.at[g], slabs[1 - g][:CH], g, weight_t)

    def fill_group(t):
        keeps = [keep_row(flags, t, cell, cell) for cell in (2 * t + 2, 2 * t + 3)]
        return fill_steps(
            group_factor_ref.at[t], GROUP, rows_of(place_ref.at[t], 0), keeps, targets[t], True
        )

    def fill_cell(t):
        cell = 4 - t
        source_of = rows_of(place_ref.at[1 - t], t * CELL_ATOMS)
        return fill_steps(
            cell_factor_ref.at[t], CELL_ATOMS, source_of, [keep_row(flags, t, cell, cell)], targets[t]
        )

    totals = [[None] * CHUNKS for _ in range(2)]
    for step in fill_cell(0):
        step()
    interleave(product_steps(cell_ref.at[0], cell_factor_ref.at[0], totals[0]), fill_group(0))
    interleave(product_steps(group_ref.at[0], group_factor_ref.at[0], totals[0]), fill_group(1))
    interleave(product_steps(group_ref.at[1], group_factor_ref.at[1], totals[1]), fill_cell(1))
    for step in product_steps(cell_ref.at[1], cell_factor_ref.at[1], totals[1]):
        step()
    for t in range(2):
        messages_ref[t] = jnp.concatenate(totals[t], axis=1)
    rows = [
        keep_row(flags, 0, 1, 1),
        keep_row(flags, 0, 0, 5),
        keep_row(flags, 1, 6, 6),
        keep_row(flags, 1, 2, 7),
    ]
    keep_ref[...] = jnp.concatenate(rows + [jnp.zeros((4, GROUP), jnp.float32)], axis=0)
    for copy in copies:
        copy.wait()


def node_kernel(
    scale,
    near_ref,
    far_ref,
    from_pair_ref,
    from_cross_ref,
    messages_ref,
    keep_ref,
    own_place_ref,
    energy_grad_ref,
    radial_ref,
    mix_ref,
    readout_ref,
    updated_ref,
    kept_ref,
    sent_ref,
    grad_messages_ref,
    cell_factor_ref,
    merged_factor_ref,
    cell_ref,
    merged_ref,
    place_ref,
):
    even = lax.axis_index("space") % 2 == 0
    weight_t = radial_ref[...].T
    near, far = near_ref[...], far_ref[...]
    from_pair, from_cross = from_pair_ref[...], from_cross_ref[...]
    slabs = (
        jnp.where(even, from_cross, from_pair),
        jnp.where(even, far, near),
        jnp.where(even, near, far),
        jnp.where(even, from_pair, from_cross),
    )
    targets = [[slab[CH + axis : CH + axis + 1] for axis in range(3)] for slab in slabs[1:3]]

    for t in range(2):
        set_place(place_ref.at[t], slabs[3 * t])
        set_cell(cell_ref.at[t], slabs[3 * t][:CH], 1 - t, weight_t)
        set_cell(merged_ref.at[t, pl.ds(0, CH)], slabs[t][:CH], 0, weight_t)
        set_cell(merged_ref.at[t, pl.ds(CH, CH)], slabs[t + 2][:CH], 1, weight_t)

    def fill_cell(t):
        source_of = rows_of(place_ref.at[t], (1 - t) * CELL_ATOMS)
        keeps = [keep_ref[2 * t : 2 * t + 1, :]]
        return fill_steps(cell_factor_ref.at[t], CELL_ATOMS, source_of, keeps, targets[t])

    def fill_merged(t):
        places = (place_ref.at[0], own_place_ref.at[0], own_place_ref.at[1], place_ref.at[1])
        source_of = merged_rows(places[t], 0, places[t + 2], CELL_ATOMS)
        keeps = [keep_ref[2 * t + 1 : 2 * t + 2, :]]
        return fill_steps(merged_factor_ref.at[t], CELL_ATOMS, source_of, keeps, targets[t])

    totals = [
        [messages_ref[t, :, k * WIDTH : min((k + 1) * WIDTH, NY * GROUP)] for k in range(CHUNKS)]
        for t in range(2)
    ]

    def add_cell(t):
        return product_steps(cell_ref.at[t], cell_factor_ref.at[t], totals[t])

    def add_merged(t):
        return product_steps(merged_ref.at[t], merged_factor_ref.at[t], totals[t], True)

    readout = jnp.broadcast_to(readout_ref[...], (8, CH)).T[:, :1]
    mix = mix_ref[...]
    mix_t = mix.astype(jnp.float32).T.astype(jnp.bfloat16)

    for step in fill_cell(0):
        step()
    interleave(add_cell(0), fill_merged(0))
    interleave(add_merged(0), fill_cell(1))
    interleave(add_cell(1), fill_merged(1))
    for step in add_merged(1):
        step()

    sides = [jnp.concatenate(total, axis=1) for total in totals]
    part = [
        jnp.concatenate([side[:, y * GROUP : (y + 1) * GROUP] for side in sides], axis=1)
        for y in range(NY)
    ]
    invariants = jnp.concatenate(
        [
            part[0],
            0.5 * (part[1] * part[1] + part[2] * part[2] + part[3] * part[3]),
            0.5
            * (
                part[4] * part[4]
                + part[5] * part[5]
                + part[6] * part[6]
                + part[7] * part[7]
                + part[8] * part[8]
            ),
        ],
        axis=0,
    ).astype(jnp.bfloat16)
    preact = jnp.dot(mix_t, invariants, preferred_element_type=jnp.float32)
    gating = jax.nn.sigmoid(preact)
    energy_grad = energy_grad_ref[...]
    spread = readout * energy_grad
    grad_pre = (spread * gating * (1.0 + preact * (1.0 - gating))).astype(jnp.bfloat16)
    grad_inv = jnp.dot(mix, grad_pre, preferred_element_type=jnp.float32)
    grad_mix = scale * lax.dot_general(
        invariants, grad_pre, (((1,), (1,)), ((), ())), preferred_element_type=jnp.float32
    )
    kept_ref[...] = jnp.where(even, grad_mix[:HALF], grad_mix[HALF:])
    sent_ref[...] = jnp.where(even, grad_mix[HALF:], grad_mix[:HALF])
    for y in range(NY):
        order = 0 if y == 0 else 1 if y < 4 else 2
        grad = grad_inv[order * CH : (order + 1) * CH]
        grad = (grad if y == 0 else grad * part[y]).astype(jnp.bfloat16)
        for t in range(2):
            grad_messages_ref[t, :, y * GROUP : (y + 1) * GROUP] = grad[:, t * GROUP : (t + 1) * GROUP]

    updated_ref[...] = jnp.concatenate([slabs[1][:CH], slabs[2][:CH]], axis=1) + preact * gating


def back(factor, grad_messages):
    return lax.dot_general(
        factor, grad_messages, (((1,), (1,)), ((), ())), preferred_element_type=jnp.float32
    )


def source_grads(total, features_t, weight):
    size = features_t.shape[0]
    grad_t = None
    radial = []
    for b in range(NB):
        piece = total[b * size : (b + 1) * size]
        term = piece * weight[b : b + 1, :]
        grad_t = term if grad_t is None else grad_t + term
        radial.append(jnp.sum(piece * features_t, axis=0, keepdims=True))
    return grad_t, jnp.concatenate(radial, axis=0)


def halo_back_kernel(
    cell_factor_ref,
    merged_factor_ref,
    grad_messages_ref,
    near_ref,
    far_ref,
    from_pair_ref,
    from_cross_ref,
    radial_ref,
    to_pair_ref,
    to_cross_ref,
    extra_ref,
    share_ref,
):
    even = lax.axis_index("space") % 2 == 0
    weight = radial_ref[...]
    near, far = near_ref[:CH, :], far_ref[:CH, :]
    from_pair, from_cross = from_pair_ref[:CH, :], from_cross_ref[:CH, :]
    features_t = [
        jnp.where(even, one, two).T
        for one, two in ((from_cross, from_pair), (far, near), (near, far), (from_pair, from_cross))
    ]
    first = lax.broadcasted_iota(jnp.int32, (CH, NY * GROUP), 1) % GROUP < CELL_ATOMS
    low, high = slice(CELL_ATOMS), slice(CELL_ATOMS, GROUP)
    share = None
    grads = {}
    for t in range(2):
        grad = grad_messages_ref[t]
        none = jnp.zeros_like(grad)
        both = jnp.concatenate([jnp.where(first, grad, none), jnp.where(first, none, grad)], axis=0)
        merged = back(merged_factor_ref[t], both)
        pieces = (
            (3 * t, 1 - t, back(cell_factor_ref[t], grad)),
            (t, 0, merged[:, :CH]),
            (t + 2, 1, merged[:, CH:]),
        )
        for g, half, total in pieces:
            grads[g, half], part = source_grads(total, features_t[g][(low, high)[half]], weight)
            share = part if share is None else share + part
    grad_before = jnp.concatenate([grads[0, 0], grads[0, 1]], axis=0).T
    grad_after = jnp.concatenate([grads[3, 0], grads[3, 1]], axis=0).T
    to_pair_ref[...] = jnp.where(even, grad_after, grad_before)
    to_cross_ref[...] = jnp.where(even, grad_before, grad_after)
    extra_ref[low, :] = grads[1, 0]
    extra_ref[high, :] = grads[2, 1]
    share_ref[...] = share


def own_back_kernel(
    scale,
    group_factor_ref,
    cell_factor_ref,
    grad_messages_ref,
    near_ref,
    far_ref,
    radial_ref,
    extra_ref,
    share_ref,
    updated_ref,
    species_ref,
    shift_ref,
    energy_grad_ref,
    readout_ref,
    own_grad_ref,
    joined_ref,
    energy_ref,
):
    even = lax.axis_index("space") % 2 == 0
    weight = radial_ref[...]
    near, far = near_ref[:CH, :], far_ref[:CH, :]
    share = share_ref[...]
    low, high = slice(CELL_ATOMS), slice(CELL_ATOMS, GROUP)
    readout = jnp.broadcast_to(readout_ref[...], (8, CH)).T[:, :1]
    updated, energy_grad, kinds = updated_ref[...], energy_grad_ref[...], species_ref[...]
    spread = readout * energy_grad
    shifts = jnp.zeros((1, 2 * GROUP), jnp.float32)
    for n in range(NSPEC):
        shifts = jnp.where(kinds == n, shift_ref[:, n : n + 1], shifts)
    energy_ref[...] = jnp.sum(updated * readout, axis=0, keepdims=True) + shifts
    readout_row = column_to_row(jnp.sum(updated * energy_grad, axis=1, keepdims=True), CH)
    here = lax.broadcasted_iota(jnp.int32, (NSPEC, 2 * GROUP), 0) == kinds
    by_kind = jnp.sum(jnp.where(here, energy_grad, 0.0), axis=1, keepdims=True)
    for t, features in enumerate((jnp.where(even, far, near), jnp.where(even, near, far))):
        features_t = features.T
        total = back(group_factor_ref[t], grad_messages_ref[t])
        grad, part = source_grads(total, features_t, weight)
        inner, outer = (high, low) if t == 0 else (low, high)
        total = back(cell_factor_ref[1 - t], grad_messages_ref[1 - t])
        one, more = source_grads(total, features_t[inner], weight)
        two = extra_ref[outer, :]
        grad = (grad + jnp.concatenate([two, one] if t == 0 else [one, two], axis=0)).T
        at = slice(t * GROUP, (t + 1) * GROUP)
        own_grad_ref[:, at] = spread[:, at] + grad
        share = share + part + more
    joined_ref[:NB, :] = share * scale
    rest = [readout_row, column_to_row(by_kind, NSPEC), jnp.zeros((6, CH), jnp.float32)]
    joined_ref[NB:, :] = jnp.concatenate(rest, axis=0) * scale


def quarter_kernel(kept_ref, received_ref, keep_ref, send_ref):
    first = first_of_pair()
    low = kept_ref[:QUARTER, :] + received_ref[:QUARTER, :]
    high = kept_ref[QUARTER:, :] + received_ref[QUARTER:, :]
    keep_ref[...] = jnp.where(first, low, high)
    send_ref[...] = jnp.where(first, high, low)


def join_kernel(kept_ref, received_ref, rest_ref, out_ref):
    out_ref[:QUARTER, :] = kept_ref[...] + received_ref[...]
    out_ref[QUARTER:, :] = rest_ref[...]


def gather_kernel(mine_ref, along_ref, other_ref, both_ref, out_ref):
    first = first_of_pair()
    at, rest = slice(QUARTER), slice(QUARTER, QUARTER + REST)
    mine = mine_ref[at, :] + along_ref[at, :]
    other = other_ref[at, :] + both_ref[at, :]
    out_ref[:QUARTER, :] = jnp.where(first, mine, other)
    out_ref[QUARTER:HALF, :] = jnp.where(first, other, mine)
    out_ref[HALF:, :] = (mine_ref[rest, :] + along_ref[rest, :]) + (other_ref[rest, :] + both_ref[rest, :])


def fold_kernel(own_ref, from_pair_ref, from_cross_ref, energy_in_ref, grad_ref, energy_ref):
    even = lax.axis_index("space") % 2 == 0
    pair = from_pair_ref[...]
    cross = from_cross_ref[...]
    grad_ref[0, :, :GROUP] = own_ref[:, :GROUP] + jnp.where(even, cross, pair)
    grad_ref[0, :, GROUP:] = own_ref[:, GROUP:] + jnp.where(even, pair, cross)
    energy_ref[...] = energy_in_ref[...]


def finish_kernel(mine_ref, other_ref, radial_ref, mix_ref, readout_ref, shift_ref):
    even = lax.axis_index("space") % 2 == 0
    mine, other = mine_ref[:HALF, :], other_ref[:HALF, :]
    mix_ref[:HALF, :] = jnp.where(even, mine, other)
    mix_ref[HALF:, :] = jnp.where(even, other, mine)
    rest = mine_ref[HALF:, :] + other_ref[HALF:, :]
    radial_ref[...] = rest[:NB]
    readout_ref[...] = rest[NB : NB + 1]
    shift_ref[...] = rest[NB + 1 : NB + 2, :NSPEC]


def first_of_pair():
    space, dp = lax.axis_index("space"), lax.axis_index("dp")
    return jnp.where(space % 2 == 0, dp, space // 2) % 2 == 0


def exchange_routes(space, dp):
    along = [(0, 1 << k) for k in range(dp.bit_length() - 1)]
    across = [(1 << k, 0) for k in range(1, space.bit_length() - 1)]
    shared = (along[0], across[0])
    orders = (across + along[1:], along[:1] + across[1:] + along[1:])
    orders = (orders[0][:-2] + orders[0][:-3:-1], orders[1])
    count = len(orders[0])

    def route(*places):
        moves = []
        for s in range(space):
            step = [shared[s % 2] if k < 0 else orders[s % 2][k] for k in places]
            for d in range(dp):
                to_s, to_d = s, d
                for one, two in step:
                    to_s, to_d = to_s ^ one, to_d ^ two
                moves.append((s * dp + d, to_s * dp + to_d))
        return moves

    rounds = []
    for k in range(0, count - 1, 2):
        if k + 1 < count - 1:
            rounds.append([route(k), route(k + 1), route(k, k + 1)])
        else:
            rounds.append([route(k)])
    last = count - 1
    rounds.append([route(last), route(-1), route(last, -1)])
    return route(-1), rounds


def call(kernel, name, inputs, outputs, mib=4, scratch=(), flops=0):
    vmem = pl.BlockSpec(memory_space=pltpu.VMEM)
    shapes = tuple(jax.ShapeDtypeStruct(shape, kind) for shape, kind in outputs)
    moved = sum(math.prod(v.shape) * v.dtype.itemsize for v in (*inputs, *shapes))
    return pl.pallas_call(
        kernel,
        out_shape=shapes,
        in_specs=[vmem] * len(inputs),
        out_specs=(vmem,) * len(shapes),
        scratch_shapes=scratch,
        compiler_params=pltpu.CompilerParams(vmem_limit_bytes=mib * 1024 * 1024),
        cost_estimate=pl.CostEstimate(flops=flops, bytes_accessed=moved, transcendentals=0),
        name=name,
    )(*inputs)


def in_hbm(value):
    return pltpu.with_memory_space_constraint(value, pltpu.HBM)


def body(
    node_features,
    positions,
    species,
    energy_cotangent,
    pair_target,
    pair_source,
    pair_count,
    radial_weight,
    mix_weight,
    readout_weight,
    species_shift,
):
    atoms_here = node_features.shape[2]
    space, dp = lax.axis_size("space"), lax.axis_size("dp")
    scale = 1.0 / math.sqrt(atoms_here * space * dp)
    pair = [(i, i ^ 1) for i in range(space)]
    cross = [(i, ((i + 1) ^ 1) - 1) for i in range(1, space - 1)]
    hbm = pl.BlockSpec(memory_space=pltpu.HBM)
    smem = pl.BlockSpec(memory_space=pltpu.SMEM)
    vmem = pl.BlockSpec(memory_space=pltpu.VMEM)
    f32, bf16 = jnp.float32, jnp.bfloat16
    small = (pair_target, pair_source, radial_weight)
    later = (
        species,
        species_shift.reshape(1, NSPEC),
        energy_cotangent,
        mix_weight,
        readout_weight.reshape(1, CH),
    )
    near, far, *small = pl.pallas_call(
        split_kernel,
        out_shape=(jax.ShapeDtypeStruct((SLAB_ROWS, GROUP), f32),) * 2
        + tuple(jax.ShapeDtypeStruct(v.shape, v.dtype) for v in small),
        in_specs=[hbm] * (SMALL + 2),
        out_specs=(vmem,) * (SMALL + 2),
        scratch_shapes=[
            pltpu.VMEM((3, 1, atoms_here), f32),
            pltpu.SemaphoreType.DMA((SMALL + 3,)),
        ],
        compiler_params=pltpu.CompilerParams(vmem_limit_bytes=4 * 1024 * 1024),
        name="split",
    )(
        in_hbm(node_features),
        in_hbm(jnp.transpose(positions, (1, 0, 2))),
        *[in_hbm(v) for v in small],
    )
    targets, sources, radial = small
    from_cross = lax.ppermute(far, "space", cross)
    from_pair = lax.ppermute(near, "space", pair)

    block_flops = 2 * CH * NB * NY * GROUP * GROUP
    group_factor, cell_factor, messages, keep, place, *later = pl.pallas_call(
        local_kernel,
        out_shape=(
            jax.ShapeDtypeStruct((2, NB * GROUP, NY * GROUP), bf16),
            jax.ShapeDtypeStruct((2, NB * CELL_ATOMS, NY * GROUP), bf16),
            jax.ShapeDtypeStruct((2, CH, NY * GROUP), f32),
            jax.ShapeDtypeStruct((8, GROUP), f32),
            jax.ShapeDtypeStruct((2, 3, GROUP, GROUP), f32),
            *[jax.ShapeDtypeStruct(v.shape, v.dtype) for v in later],
        ),
        in_specs=[smem] + [vmem] * 5 + [hbm] * LATER,
        out_specs=(vmem,) * (5 + LATER),
        scratch_shapes=[
            pltpu.VMEM((2, CH, NB * GROUP), bf16),
            pltpu.VMEM((2, CH, NB * CELL_ATOMS), bf16),
            pltpu.SemaphoreType.DMA((LATER,)),
        ],
        compiler_params=pltpu.CompilerParams(vmem_limit_bytes=16 * 1024 * 1024),
        cost_estimate=pl.CostEstimate(
            flops=3 * block_flops, bytes_accessed=11_000_000, transcendentals=0
        ),
        name="local_pairs",
    )(pair_count, targets, sources, radial, near, far, *[in_hbm(v) for v in later])
    species, shift, energy_grad, mix, readout = later

    updated, kept, sent, grad_messages, halo_factor, merged_factor = call(
        functools.partial(node_kernel, scale),
        "node_stage",
        (
            near,
            far,
            from_pair,
            from_cross,
            messages,
            keep,
            place,
            energy_grad,
            radial,
            mix,
            readout,
        ),
        (
            ((CH, atoms_here), f32),
            ((HALF, CH), f32),
            ((HALF, CH), f32),
            ((2, CH, NY * GROUP), bf16),
            ((2, NB * CELL_ATOMS, NY * GROUP), bf16),
            ((2, NB * CELL_ATOMS, NY * GROUP), bf16),
        ),
        16,
        [
            pltpu.VMEM((2, CH, NB * CELL_ATOMS), bf16),
            pltpu.VMEM((2, 2 * CH, NB * CELL_ATOMS), bf16),
            pltpu.VMEM((2, 3, GROUP, GROUP), f32),
        ],
        2 * block_flops,
    )

    received = lax.ppermute(sent, "space", pair)
    pair_grad, cross_grad, extra, share = call(
        halo_back_kernel,
        "halo_back",
        (
            halo_factor,
            merged_factor,
            grad_messages,
            near,
            far,
            from_pair,
            from_cross,
            radial,
        ),
        (((CH, GROUP), f32), ((CH, GROUP), f32), ((GROUP, CH), f32), ((NB, CH), f32)),
        12,
        (),
        2 * block_flops,
    )
    received, share = lax.optimization_barrier((received, share))
    quarter, sent = call(
        quarter_kernel,
        "quarter",
        (kept, received),
        (((QUARTER, CH), f32), ((QUARTER, CH), f32)),
    )
    sharing, (*rounds, last) = exchange_routes(space, dp)
    everyone = ("space", "dp")
    sent, grad_messages, pair_grad = lax.optimization_barrier((sent, grad_messages, pair_grad))
    received = lax.ppermute(sent, everyone, sharing)
    from_pair = lax.ppermute(pair_grad, "space", pair)
    own_grad, joined, energy = call(
        functools.partial(own_back_kernel, scale),
        "own_back",
        (
            group_factor,
            cell_factor,
            grad_messages,
            near,
            far,
            radial,
            extra,
            share,
            updated,
            species,
            shift,
            energy_grad,
            readout,
        ),
        (((CH, atoms_here), f32), ((REST, CH), f32), ((1, atoms_here), f32)),
        12,
        (),
        3 * block_flops,
    )
    (value,) = call(
        join_kernel, "join", (quarter, received, joined), (((QUARTER + REST, CH), f32),)
    )
    value, from_pair, cross_grad = lax.optimization_barrier((value, from_pair, cross_grad))
    for turn, routes in enumerate(rounds):
        arrived = [lax.ppermute(value, everyone, route) for route in routes]
        if turn == 0:
            from_cross = lax.ppermute(cross_grad, "space", cross)
        value = value + arrived[0]
        if len(arrived) == 3:
            value = value + (arrived[1] + arrived[2])
    arrived = [lax.ppermute(value, everyone, route) for route in last]
    value, from_cross, *arrived = lax.optimization_barrier((value, from_cross, *arrived))
    (value,) = call(
        gather_kernel,
        "gather",
        (value, *arrived),
        (((HALF + REST, CH), f32),),
    )
    feature_grad, energy = call(
        fold_kernel,
        "fold",
        (own_grad, from_pair, from_cross, energy),
        (((1, CH, atoms_here), f32), ((1, atoms_here), f32)),
    )
    radial_grad, mix_grad, readout_grad, shift_grad = call(
        finish_kernel,
        "finish",
        (value, lax.ppermute(value, "space", pair)),
        (((NB, CH), f32), ((MIX_ROWS, CH), f32), ((1, CH), f32), ((1, NSPEC), f32)),
    )
    return (
        energy,
        feature_grad,
        radial_grad,
        mix_grad,
        readout_grad.reshape(CH),
        shift_grad.reshape(NSPEC),
    )


def solution(mesh):
    return jax.shard_map(
        body,
        mesh=mesh,
        in_specs=(
            P("dp", None, "space"),
            P("dp", None, "space"),
            P("dp", "space"),
            P("dp", "space"),
            P("dp", "space"),
            P("dp", "space"),
            P("dp", "space"),
            P(),
            P(),
            P(),
            P(),
        ),
        out_specs=(P("dp", "space"), P("dp", None, "space"), P(), P(), P(), P()),
        check_vma=False,
    )
```

profile of v0, /device:TPU:0, one launch (start us, length us, event | category | flops | bytes accessed | tf_op | source)
XLA Modules:
  0.0 37.6 jit_solution(10953497807432110097)
XLA Ops:
  0.6 0.9 %split.1 = (f32[136,128]{1,0:T(8,128)S(1)}, f32[136,128]{1,0:T(8,128)S(1)}, s32[1,20]{1,0:T(1,128)S(1)}, s32[1,20]{1,0:T(1,128)S(1)}, f32[8,128]{1,0:T(8,128)S(1)}) custom-call(f32[1,128,256]{2,1,0:T(8,128)} %refs_0_.2, f32[3,1,256]{2,1,0:T(1,128)} %bitcast.5, s32[1,20]{1,0:T(1,128)} %refs_2_.1, s32[1,20]{1,0:T(1,128)} %refs_3_.1, f32[8,128]{1,0:T(8,128)} %refs_4_.1), custom_call_target="tpu_custom_call" | custom-call | tf_op jit(solution)/shard_map/split/pallas_call | solution.py:639
  1.6 0.5 %collective-permute-start = (f32[136,128]{1,0:T(8,128)S(1)}, f32[136,128]{1,0:T(8,128)S(1)}, u32[]{:S(2)}, u32[]{:S(2)}) collective-permute-start(f32[136,128]{1,0:T(8,128)S(1)} %get-tuple-element.58.refs_4_.near_ref), channel_id=1, source_target_pairs={{0,2},{2,0},{4,6},{6,4},{8,10},{10,8},{12,14},{14,12},{16,18},{18,... | collective-permute-start | bytes 208904 | tf_op jit(solution)/shard_map/ppermute | solution.py:658
  2.1 0.7 %collective-permute-start.1 = (f32[136,128]{1,0:T(8,128)S(1)}, f32[136,128]{1,0:T(8,128)S(1)}, u32[]{:S(2)}, u32[]{:S(2)}) collective-permute-start(f32[136,128]{1,0:T(8,128)S(1)} %get-tuple-element.59.refs_5_.far_ref), channel_id=1, source_target_pairs={{2,4},{4,2},{6,8},{8,6},{10,12},{12,10},{14,16},{16,14},{18,20},{2... | collective-permute-start | bytes 208904 | tf_op jit(solution)/shard_map/ppermute | solution.py:657
  3.4 3.5 %local_pairs.1 = (bf16[2,1024,1152]{2,1,0:T(8,128)(2,1)S(1)}, bf16[2,512,1152]{2,1,0:T(8,128)(2,1)S(1)}, f32[2,128,1152]{2,1,0:T(8,128)S(1)}, f32[8,128]{1,0:T(8...) custom-call(s32[1,1]{1,0:T(1,128)S(6)} %copy.17.refs_0_, ...), custom_call_target="tpu_custom_call" | custom-call | flops 905969664 | bytes 11000000 | tf_op jit(solution)/shard_map/local_pairs/pallas_call | solution.py:661
  6.9 0.0 collective-permute-done.from_pair_ref
  6.9 0.0 collective-permute-done.1.from_cross_ref
  6.9 3.0 %node_stage.1 = (f32[128,256]{1,0:T(8,128)S(1)}, f32[192,128]{1,0:T(8,128)S(1)}, f32[192,128]{1,0:T(8,128)S(1)}, bf16[2,128,1152]{2,1,0:T(8,128)(2,1)S(1)}, bf16...) custom-call(f32[136,128]{1,0:T(8,128)S(1)} %get-tuple-element.58.refs_4_.near_ref, ...), custom_call_target="tpu_custom_call" | custom-call | flops 603979776 | bytes 7595520 | tf_op jit(solution)/shard_map/node_stage/pallas_call | solution.py:593
  10.0 4.0 %collective-permute-start.2 = (f32[192,128]{1,0:T(8,128)S(1)}, f32[192,128]{1,0:T(8,128)S(1)}, u32[]{:S(2)}, u32[]{:S(2)}) collective-permute-start(f32[192,128]{1,0:T(8,128)S(1)} %get-tuple-element.69), channel_id=1, source_target_pairs={{0,2},{2,0},{4,6},{6,4},{8,10},{10,8},{12,14},{14,12},{16,18},{18,... | collective-permute-start | bytes 294920 | tf_op jit(solution)/shard_map/ppermute | solution.py:719
  13.9 1.6 %halo_back.1 = (f32[128,128]{1,0:T(8,128)S(1)}, f32[128,128]{1,0:T(8,128)S(1)}, f32[128,128]{1,0:T(8,128)S(1)}, f32[8,128]{1,0:T(8,128)S(1)}) custom-call(bf16[2,512,1152]{2,1,0:T(8,128)(2,1)S(1)} %get-tuple-element.70.cell_factor_ref, bf16[2,512,1152]{2,1,0:T(8,128)(2,1)S(1)} %get-tuple-element.71.merged_factor_ref, ...), custom_call_target="tpu_custom_call" | custom-call | flops 603979776 | bytes 5791744 | tf_op jit(solution)/shard_map/halo_back/pallas_call | solution.py:593
  15.5 0.0 collective-permute-done.2.received_ref
  15.6 1.6 %collective-permute-start.3 = (f32[96,128]{1,0:T(8,128)S(1)}, f32[96,128]{1,0:T(8,128)S(1)}, u32[]{:S(2)}, u32[]{:S(2)}) collective-permute-start(f32[96,128]{1,0:T(8,128)S(1)} %get-tuple-element.85), channel_id=1, source_target_pairs={{0,1},{1,0},{2,6},{3,7},{4,5},{5,4},{6,2},{7,3},{8,9},{9,8},{10,14... | collective-permute-start | bytes 147464 | tf_op jit(solution)/shard_map/ppermute | solution.py:748
  17.1 0.0 collective-permute-start.4
  17.1 2.2 %own_back.1 = (f32[128,256]{1,0:T(8,128)S(1)}, f32[16,128]{1,0:T(8,128)S(1)}, f32[1,256]{1,0:T(1,128)S(1)}) custom-call(bf16[2,1024,1152]{2,1,0:T(8,128)(2,1)S(1)} %get-tuple-element.60.group_factor_ref, bf16[2,512,1152]{2,1,0:T(8,128)(2,1)S(1)} %get-tuple-element.61.cell_factor_ref, bf16[2,128,1152]{2,1,0:T(8,128)(2,1)S(1)} %get-tuple-element.77.grad_messages_ref, ...), custom_call_target="tpu_custom_call" | custom-call | flops 905969664 | bytes 8154656 | tf_op jit(solution)/shard_map/own_back/pallas_call | solution.py:593
  19.3 0.4 %collective-permute-done.3.received_ref = f32[96,128]{1,0:T(8,128)S(1)} collective-permute-done((f32[96,128]{1,0:T(8,128)S(1)}, f32[96,128]{1,0:T(8,128)S(1)}, u32[]{:S(2)}, u32[]{:S(2)}) %collective-permute-start.3) | collective-permute-done | bytes 49184 | tf_op jit(solution)/shard_map/ppermute | solution.py:748
  19.7 0.0 collective-permute-done.4.from_pair_ref
  19.7 3.6 %collective-permute-start.7 = (f32[112,128]{1,0:T(8,128)S(1)}, f32[112,128]{1,0:T(8,128)S(1)}, u32[]{:S(2)}, u32[]{:S(2)}) collective-permute-start(f32[112,128]{1,0:T(8,128)S(1)} %join.1), channel_id=1, source_target_pairs={{0,20},{1,21},{2,11},{3,10},{4,16},{5,17},{6,15},{7,14},{8,28},{9,... | collective-permute-start | bytes 172040 | tf_op jit(solution)/shard_map/ppermute | solution.py:778
  23.3 0.3 collective-permute-start.6
  23.7 0.5 %collective-permute-start.5 = (f32[112,128]{1,0:T(8,128)S(1)}, f32[112,128]{1,0:T(8,128)S(1)}, u32[]{:S(2)}, u32[]{:S(2)}) collective-permute-start(f32[112,128]{1,0:T(8,128)S(1)} %join.1), channel_id=1, source_target_pairs={{0,4},{1,5},{2,3},{3,2},{4,0},{5,1},{6,7},{7,6},{8,12},{9,13},{10,... | collective-permute-start | bytes 172040 | tf_op jit(solution)/shard_map/ppermute | solution.py:778
  24.2 0.7 %collective-permute-start.8 = (f32[128,128]{1,0:T(8,128)S(1)}, f32[128,128]{1,0:T(8,128)S(1)}, u32[]{:S(2)}, u32[]{:S(2)}) collective-permute-start(f32[128,128]{1,0:T(8,128)S(1)} %get-tuple-element.91), channel_id=1, source_target_pairs={{2,4},{4,2},{6,8},{8,6},{10,12},{12,10},{14,16},{16,14},{18,20},{2... | collective-permute-start | bytes 196616 | tf_op jit(solution)/shard_map/ppermute | solution.py:780
  24.9 1.0 %collective-permute-done.7 = f32[112,128]{1,0:T(8,128)S(1)} collective-permute-done((f32[112,128]{1,0:T(8,128)S(1)}, f32[112,128]{1,0:T(8,128)S(1)}, u32[]{:S(2)}, u32[]{:S(2)}) %collective-permute-start.7) | collective-permute-done | bytes 57376 | tf_op jit(solution)/shard_map/ppermute | solution.py:778
  25.9 3.1 %collective-permute-done.6 = f32[112,128]{1,0:T(8,128)S(1)} collective-permute-done((f32[112,128]{1,0:T(8,128)S(1)}, f32[112,128]{1,0:T(8,128)S(1)}, u32[]{:S(2)}, u32[]{:S(2)}) %collective-permute-start.6) | collective-permute-done | bytes 57376 | tf_op jit(solution)/shard_map/ppermute | solution.py:778
  29.0 0.0 collective-permute-done.5
  29.1 1.4 %collective-permute-start.11 = (f32[112,128]{1,0:T(8,128)S(1)}, f32[112,128]{1,0:T(8,128)S(1)}, u32[]{:S(2)}, u32[]{:S(2)}) collective-permute-start(f32[112,128]{1,0:T(8,128)S(1)} %add_add_fusion.mine_ref), channel_id=1, source_target_pairs={{0,9},{1,8},{2,22},{3,23},{4,13},{5,12},{6,18},{7,19},{8,1},{9,0},... | collective-permute-start | bytes 172040 | tf_op jit(solution)/shard_map/ppermute | solution.py:784
  30.5 0.5 %collective-permute-start.10 = (f32[112,128]{1,0:T(8,128)S(1)}, f32[112,128]{1,0:T(8,128)S(1)}, u32[]{:S(2)}, u32[]{:S(2)}) collective-permute-start(f32[112,128]{1,0:T(8,128)S(1)} %add_add_fusion.mine_ref), channel_id=1, source_target_pairs={{0,1},{1,0},{2,6},{3,7},{4,5},{5,4},{6,2},{7,3},{8,9},{9,8},{10,14... | collective-permute-start | bytes 172040 | tf_op jit(solution)/shard_map/ppermute | solution.py:784
  31.0 1.6 %collective-permute-start.9 = (f32[112,128]{1,0:T(8,128)S(1)}, f32[112,128]{1,0:T(8,128)S(1)}, u32[]{:S(2)}, u32[]{:S(2)}) collective-permute-start(f32[112,128]{1,0:T(8,128)S(1)} %add_add_fusion.mine_ref), channel_id=1, source_target_pairs={{0,8},{1,9},{2,18},{3,19},{4,12},{5,13},{6,22},{7,23},{8,0},{9,1},... | collective-permute-start | bytes 172040 | tf_op jit(solution)/shard_map/ppermute | solution.py:784
  32.6 0.0 collective-permute-done.8.from_cross_ref
  32.6 1.9 %collective-permute-done.11.both_ref = f32[112,128]{1,0:T(8,128)S(1)} collective-permute-done((f32[112,128]{1,0:T(8,128)S(1)}, f32[112,128]{1,0:T(8,128)S(1)}, u32[]{:S(2)}, u32[]{:S(2)}) %collective-permute-start.11) | collective-permute-done | bytes 57376 | tf_op jit(solution)/shard_map/ppermute | solution.py:784
  34.5 0.6 %collective-permute-done.10.other_ref = f32[112,128]{1,0:T(8,128)S(1)} collective-permute-done((f32[112,128]{1,0:T(8,128)S(1)}, f32[112,128]{1,0:T(8,128)S(1)}, u32[]{:S(2)}, u32[]{:S(2)}) %collective-permute-start.10) | collective-permute-done | bytes 57376 | tf_op jit(solution)/shard_map/ppermute | solution.py:784
  35.1 0.3 collective-permute-done.9.along_ref
  35.4 0.5 %collective-permute-start.12 = (f32[208,128]{1,0:T(8,128)S(1)}, f32[208,128]{1,0:T(8,128)S(1)}, u32[]{:S(2)}, u32[]{:S(2)}) collective-permute-start(f32[208,128]{1,0:T(8,128)S(1)} %gather.1.mine_ref), channel_id=1, source_target_pairs={{0,2},{2,0},{4,6},{6,4},{8,10},{10,8},{12,14},{14,12},{16,18},{18,... | collective-permute-start | bytes 319496 | tf_op jit(solution)/shard_map/ppermute | solution.py:801
  36.0 0.7 %fold.1 = (f32[1,128,256]{2,1,0:T(8,128)}, f32[1,256]{1,0:T(1,128)}) custom-call(f32[128,256]{1,0:T(8,128)S(1)} %get-tuple-element.83.own_ref, f32[128,128]{1,0:T(8,128)S(1)} %collective-permute-done.4.from_pair_ref, f32[128,128]{1,0:T(8,128)S(1)} %collective-permute-done.8.from_cross_ref, f32[1,256]{1,0:T(1,128)S(1)} %get-tuple-element.93.energy_in_ref), custom_call_target="tpu_custom_call" | custom-call | bytes 395264 | tf_op jit(solution)/shard_map/fold/pallas_call | solution.py:593
  36.7 0.3 collective-permute-done.12.other_ref
  36.9 0.7 %finish.1 = (f32[8,128]{1,0:T(8,128)}, f32[384,128]{1,0:T(8,128)}, f32[1,128]{1,0:T(1,128)}, f32[1,8]{1,0:T(1,128)}) custom-call(f32[208,128]{1,0:T(8,128)S(1)} %gather.1.mine_ref, f32[208,128]{1,0:T(8,128)S(1)} %collective-permute-done.12.other_ref), custom_call_target="tpu_custom_call" | custom-call | bytes 414240 | tf_op jit(solution)/shard_map/finish/pallas_call | solution.py:593
  (4 shorter events, 0.1 us)
Async XLA Ops:
  1.6 5.3 %collective-permute-start = (f32[136,128]{1,0:T(8,128)S(1)}, f32[136,128]{1,0:T(8,128)S(1)}, u32[]{:S(2)}, u32[]{:S(2)}) collective-permute-start(f32[136,128]{1,0:T(8,128)S(1)} %get-tuple-element.58.refs_4_.near_ref), channel_id=1, source_target_pairs={{0,2},{2,0},{4,6},{6,4},{8,10},{10,8},{12,14},{14,12},{16,18},{18,... | collective-permute-start | bytes 208904 | tf_op jit(solution)/shard_map/ppermute | solution.py:658
  2.1 4.8 %collective-permute-start.1 = (f32[136,128]{1,0:T(8,128)S(1)}, f32[136,128]{1,0:T(8,128)S(1)}, u32[]{:S(2)}, u32[]{:S(2)}) collective-permute-start(f32[136,128]{1,0:T(8,128)S(1)} %get-tuple-element.59.refs_5_.far_ref), channel_id=1, source_target_pairs={{2,4},{4,2},{6,8},{8,6},{10,12},{12,10},{14,16},{16,14},{18,20},{2... | collective-permute-start | bytes 208904 | tf_op jit(solution)/shard_map/ppermute | solution.py:657
  10.0 5.5 %collective-permute-start.2 = (f32[192,128]{1,0:T(8,128)S(1)}, f32[192,128]{1,0:T(8,128)S(1)}, u32[]{:S(2)}, u32[]{:S(2)}) collective-permute-start(f32[192,128]{1,0:T(8,128)S(1)} %get-tuple-element.69), channel_id=1, source_target_pairs={{0,2},{2,0},{4,6},{6,4},{8,10},{10,8},{12,14},{14,12},{16,18},{18,... | collective-permute-start | bytes 294920 | tf_op jit(solution)/shard_map/ppermute | solution.py:719
  15.6 4.2 %collective-permute-start.3 = (f32[96,128]{1,0:T(8,128)S(1)}, f32[96,128]{1,0:T(8,128)S(1)}, u32[]{:S(2)}, u32[]{:S(2)}) collective-permute-start(f32[96,128]{1,0:T(8,128)S(1)} %get-tuple-element.85), channel_id=1, source_target_pairs={{0,1},{1,0},{2,6},{3,7},{4,5},{5,4},{6,2},{7,3},{8,9},{9,8},{10,14... | collective-permute-start | bytes 147464 | tf_op jit(solution)/shard_map/ppermute | solution.py:748
  17.1 2.6 %collective-permute-start.4 = (f32[128,128]{1,0:T(8,128)S(1)}, f32[128,128]{1,0:T(8,128)S(1)}, u32[]{:S(2)}, u32[]{:S(2)}) collective-permute-start(f32[128,128]{1,0:T(8,128)S(1)} %get-tuple-element.87), channel_id=1, source_target_pairs={{0,2},{2,0},{4,6},{6,4},{8,10},{10,8},{12,14},{14,12},{16,18},{18,... | collective-permute-start | bytes 196616 | tf_op jit(solution)/shard_map/ppermute | solution.py:749
  19.7 6.1 %collective-permute-start.7 = (f32[112,128]{1,0:T(8,128)S(1)}, f32[112,128]{1,0:T(8,128)S(1)}, u32[]{:S(2)}, u32[]{:S(2)}) collective-permute-start(f32[112,128]{1,0:T(8,128)S(1)} %join.1), channel_id=1, source_target_pairs={{0,20},{1,21},{2,11},{3,10},{4,16},{5,17},{6,15},{7,14},{8,28},{9,... | collective-permute-start | bytes 172040 | tf_op jit(solution)/shard_map/ppermute | solution.py:778
  23.3 5.7 %collective-permute-start.6 = (f32[112,128]{1,0:T(8,128)S(1)}, f32[112,128]{1,0:T(8,128)S(1)}, u32[]{:S(2)}, u32[]{:S(2)}) collective-permute-start(f32[112,128]{1,0:T(8,128)S(1)} %join.1), channel_id=1, source_target_pairs={{0,16},{1,17},{2,10},{3,11},{4,20},{5,21},{6,14},{7,15},{8,24},{9,... | collective-permute-start | bytes 172040 | tf_op jit(solution)/shard_map/ppermute | solution.py:778
  23.7 5.4 %collective-permute-start.5 = (f32[112,128]{1,0:T(8,128)S(1)}, f32[112,128]{1,0:T(8,128)S(1)}, u32[]{:S(2)}, u32[]{:S(2)}) collective-permute-start(f32[112,128]{1,0:T(8,128)S(1)} %join.1), channel_id=1, source_target_pairs={{0,4},{1,5},{2,3},{3,2},{4,0},{5,1},{6,7},{7,6},{8,12},{9,13},{10,... | collective-permute-start | bytes 172040 | tf_op jit(solution)/shard_map/ppermute | solution.py:778
  24.2 8.4 %collective-permute-start.8 = (f32[128,128]{1,0:T(8,128)S(1)}, f32[128,128]{1,0:T(8,128)S(1)}, u32[]{:S(2)}, u32[]{:S(2)}) collective-permute-start(f32[128,128]{1,0:T(8,128)S(1)} %get-tuple-element.91), channel_id=1, source_target_pairs={{2,4},{4,2},{6,8},{8,6},{10,12},{12,10},{14,16},{16,14},{18,20},{2... | collective-permute-start | bytes 196616 | tf_op jit(solution)/shard_map/ppermute | solution.py:780
  29.1 5.4 %collective-permute-start.11 = (f32[112,128]{1,0:T(8,128)S(1)}, f32[112,128]{1,0:T(8,128)S(1)}, u32[]{:S(2)}, u32[]{:S(2)}) collective-permute-start(f32[112,128]{1,0:T(8,128)S(1)} %add_add_fusion.mine_ref), channel_id=1, source_target_pairs={{0,9},{1,8},{2,22},{3,23},{4,13},{5,12},{6,18},{7,19},{8,1},{9,0},... | collective-permute-start | bytes 172040 | tf_op jit(solution)/shard_map/ppermute | solution.py:784
  30.5 4.6 %collective-permute-start.10 = (f32[112,128]{1,0:T(8,128)S(1)}, f32[112,128]{1,0:T(8,128)S(1)}, u32[]{:S(2)}, u32[]{:S(2)}) collective-permute-start(f32[112,128]{1,0:T(8,128)S(1)} %add_add_fusion.mine_ref), channel_id=1, source_target_pairs={{0,1},{1,0},{2,6},{3,7},{4,5},{5,4},{6,2},{7,3},{8,9},{9,8},{10,14... | collective-permute-start | bytes 172040 | tf_op jit(solution)/shard_map/ppermute | solution.py:784
  31.0 4.4 %collective-permute-start.9 = (f32[112,128]{1,0:T(8,128)S(1)}, f32[112,128]{1,0:T(8,128)S(1)}, u32[]{:S(2)}, u32[]{:S(2)}) collective-permute-start(f32[112,128]{1,0:T(8,128)S(1)} %add_add_fusion.mine_ref), channel_id=1, source_target_pairs={{0,8},{1,9},{2,18},{3,19},{4,12},{5,13},{6,22},{7,23},{8,0},{9,1},... | collective-permute-start | bytes 172040 | tf_op jit(solution)/shard_map/ppermute | solution.py:784
  35.4 1.5 %collective-permute-start.12 = (f32[208,128]{1,0:T(8,128)S(1)}, f32[208,128]{1,0:T(8,128)S(1)}, u32[]{:S(2)}, u32[]{:S(2)}) collective-permute-start(f32[208,128]{1,0:T(8,128)S(1)} %gather.1.mine_ref), channel_id=1, source_target_pairs={{0,2},{2,0},{4,6},{6,4},{8,10},{10,8},{12,14},{14,12},{16,18},{18,... | collective-permute-start | bytes 319496 | tf_op jit(solution)/shard_map/ppermute | solution.py:801
where the time goes:
time: 37.8 us; the launch traced here: 37.6 us
  starting transfers between devices  15.9 us (42%)
  Pallas kernels  12.7 us (34%)
  waiting for transfers between devices  7.68 us (20%)
  between operations  1.4 us (4%)
    pallas_call x8, Pallas kernels, call(): pl.pallas_call(kernel, out_shape=shapes, in_specs=[vmem] * len(inputs), o...  8.22 us
    ppermute x3, starting transfers between devices, body(): arrived = [lax.ppermute(value, everyone, route) for route in routes]  4.45 us
    ppermute x3, waiting for transfers between devices, body(): arrived = [lax.ppermute(value, everyone, route) for route in routes]  4.18 us
    ppermute x1, starting transfers between devices, body(): received = lax.ppermute(sent, 'space', pair)  3.97 us
    ppermute x3, starting transfers between devices, body(): arrived = [lax.ppermute(value, everyone, route) for route in last]  3.55 us
    pallas_call x1, Pallas kernels, body(): pl.pallas_call(local_kernel, out_shape=(jax.ShapeDtypeStruct((2, NB * GRO...  3.48 us
    ppermute x3, waiting for transfers between devices, body(): arrived = [lax.ppermute(value, everyone, route) for route in last]  2.79 us
    ppermute x1, starting transfers between devices, body(): received = lax.ppermute(sent, everyone, sharing)  1.56 us
  transfers between devices with their start and end apart: 13, of which 7 were waited for; matrix products, arithmetic and copies ran while one was open for 0% of the time, Pallas kernels for 21%

commit v1 on v0

--- a/solution.py
+++ b/solution.py
@@ -561,7 +561,7 @@
     across = [(1 << k, 0) for k in range(1, space.bit_length() - 1)]
     shared = (along[0], across[0])
     orders = (across + along[1:], along[:1] + across[1:] + along[1:])
-    orders = (orders[0][:-2] + orders[0][:-3:-1], orders[1])
+    orders = (orders[0], orders[1][:-2] + orders[1][:-3:-1])
     count = len(orders[0])
 
     def route(*places):

time: 37.8 us -> 39.1 us (1.034)
  waiting for transfers between devices: 7.68 us -> 9.39 us
  starting transfers between devices: 15.9 us -> 15.4 us
    ppermute x3, waiting for transfers between devices: 2.79 us -> 5.19 us  [body(): arrived = [lax.ppermute(value, everyone, route) for route in last]]
    ppermute x3, waiting for transfers between devices: 4.18 us -> 3.16 us  [body(): arrived = [lax.ppermute(value, everyone, route) for route in routes]]
    ppermute x3, starting transfers between devices: 3.55 us -> 4.45 us  [body(): arrived = [lax.ppermute(value, everyone, route) for route in last]]
    ppermute x3, starting transfers between devices: 4.45 us -> 3.55 us  [body(): arrived = [lax.ppermute(value, everyone, route) for route in routes]]
    ppermute x1, starting transfers between devices: 0.54 us -> 0.07 us  [body(): lax.ppermute(value, 'space', pair)]
  transfers between devices with their start and end apart: 13 -> 13, of which waited for: 7 -> 7; matrix products, arithmetic and copies ran while one was open for 0% -> 0% of each run, Pallas kernels for 21% -> 20%
where the time goes in v1:
time: 39.1 us; the launch traced here: 38.9 us
  starting transfers between devices  15.4 us (39%)
  Pallas kernels  12.7 us (32%)
  waiting for transfers between devices  9.39 us (24%)
  between operations  1.4 us (4%)
    pallas_call x8, Pallas kernels, call(): pl.pallas_call(kernel, out_shape=shapes, in_specs=[vmem] * len(inputs), o...  8.23 us
    ppermute x3, waiting for transfers between devices, body(): arrived = [lax.ppermute(value, everyone, route) for route in last]  5.19 us
    ppermute x3, starting transfers between devices, body(): arrived = [lax.ppermute(value, everyone, route) for route in last]  4.45 us
    ppermute x1, starting transfers between devices, body(): received = lax.ppermute(sent, 'space', pair)  3.97 us
    ppermute x3, starting transfers between devices, body(): arrived = [lax.ppermute(value, everyone, route) for route in routes]  3.55 us
    pallas_call x1, Pallas kernels, body(): pl.pallas_call(local_kernel, out_shape=(jax.ShapeDtypeStruct((2, NB * GRO...  3.48 us
    ppermute x3, waiting for transfers between devices, body(): arrived = [lax.ppermute(value, everyone, route) for route in routes]  3.16 us
    ppermute x1, starting transfers between devices, body(): received = lax.ppermute(sent, everyone, sharing)  1.56 us
  transfers between devices with their start and end apart: 13, of which 7 were waited for; matrix products, arithmetic and copies ran while one was open for 0% of the time, Pallas kernels for 20%

profile of v1, /device:TPU:0, one launch (start us, length us, event | category | flops | bytes accessed | tf_op | source)
XLA Modules:
  0.0 38.9 jit_solution(10377746215474329283)
XLA Ops:
  0.6 0.9 %split.1 = (f32[136,128]{1,0:T(8,128)S(1)}, f32[136,128]{1,0:T(8,128)S(1)}, s32[1,20]{1,0:T(1,128)S(1)}, s32[1,20]{1,0:T(1,128)S(1)}, f32[8,128]{1,0:T(8,128)S(1)}) custom-call(f32[1,128,256]{2,1,0:T(8,128)} %refs_0_.2, f32[3,1,256]{2,1,0:T(1,128)} %bitcast.5, s32[1,20]{1,0:T(1,128)} %refs_2_.1, s32[1,20]{1,0:T(1,128)} %refs_3_.1, f32[8,128]{1,0:T(8,128)} %refs_4_.1), custom_call_target="tpu_custom_call" | custom-call | tf_op jit(solution)/shard_map/split/pallas_call | solution.py:639
  1.6 0.5 %collective-permute-start = (f32[136,128]{1,0:T(8,128)S(1)}, f32[136,128]{1,0:T(8,128)S(1)}, u32[]{:S(2)}, u32[]{:S(2)}) collective-permute-start(f32[136,128]{1,0:T(8,128)S(1)} %get-tuple-element.58.refs_4_.near_ref), channel_id=1, source_target_pairs={{0,2},{2,0},{4,6},{6,4},{8,10},{10,8},{12,14},{14,12},{16,18},{18,... | collective-permute-start | bytes 208904 | tf_op jit(solution)/shard_map/ppermute | solution.py:658
  2.1 0.7 %collective-permute-start.1 = (f32[136,128]{1,0:T(8,128)S(1)}, f32[136,128]{1,0:T(8,128)S(1)}, u32[]{:S(2)}, u32[]{:S(2)}) collective-permute-start(f32[136,128]{1,0:T(8,128)S(1)} %get-tuple-element.59.refs_5_.far_ref), channel_id=1, source_target_pairs={{2,4},{4,2},{6,8},{8,6},{10,12},{12,10},{14,16},{16,14},{18,20},{2... | collective-permute-start | bytes 208904 | tf_op jit(solution)/shard_map/ppermute | solution.py:657
  3.4 3.5 %local_pairs.1 = (bf16[2,1024,1152]{2,1,0:T(8,128)(2,1)S(1)}, bf16[2,512,1152]{2,1,0:T(8,128)(2,1)S(1)}, f32[2,128,1152]{2,1,0:T(8,128)S(1)}, f32[8,128]{1,0:T(8...) custom-call(s32[1,1]{1,0:T(1,128)S(6)} %copy.17.refs_0_, ...), custom_call_target="tpu_custom_call" | custom-call | flops 905969664 | bytes 11000000 | tf_op jit(solution)/shard_map/local_pairs/pallas_call | solution.py:661
  6.9 0.0 collective-permute-done.from_pair_ref
  6.9 0.0 collective-permute-done.1.from_cross_ref
  6.9 3.0 %node_stage.1 = (f32[128,256]{1,0:T(8,128)S(1)}, f32[192,128]{1,0:T(8,128)S(1)}, f32[192,128]{1,0:T(8,128)S(1)}, bf16[2,128,1152]{2,1,0:T(8,128)(2,1)S(1)}, bf16...) custom-call(f32[136,128]{1,0:T(8,128)S(1)} %get-tuple-element.58.refs_4_.near_ref, ...), custom_call_target="tpu_custom_call" | custom-call | flops 603979776 | bytes 7595520 | tf_op jit(solution)/shard_map/node_stage/pallas_call | solution.py:593
  10.0 4.0 %collective-permute-start.2 = (f32[192,128]{1,0:T(8,128)S(1)}, f32[192,128]{1,0:T(8,128)S(1)}, u32[]{:S(2)}, u32[]{:S(2)}) collective-permute-start(f32[192,128]{1,0:T(8,128)S(1)} %get-tuple-element.69), channel_id=1, source_target_pairs={{0,2},{2,0},{4,6},{6,4},{8,10},{10,8},{12,14},{14,12},{16,18},{18,... | collective-permute-start | bytes 294920 | tf_op jit(solution)/shard_map/ppermute | solution.py:719
  13.9 1.6 %halo_back.1 = (f32[128,128]{1,0:T(8,128)S(1)}, f32[128,128]{1,0:T(8,128)S(1)}, f32[128,128]{1,0:T(8,128)S(1)}, f32[8,128]{1,0:T(8,128)S(1)}) custom-call(bf16[2,512,1152]{2,1,0:T(8,128)(2,1)S(1)} %get-tuple-element.70.cell_factor_ref, bf16[2,512,1152]{2,1,0:T(8,128)(2,1)S(1)} %get-tuple-element.71.merged_factor_ref, ...), custom_call_target="tpu_custom_call" | custom-call | flops 603979776 | bytes 5791744 | tf_op jit(solution)/shard_map/halo_back/pallas_call | solution.py:593
  15.5 0.0 collective-permute-done.2.received_ref
  15.6 1.6 %collective-permute-start.3 = (f32[96,128]{1,0:T(8,128)S(1)}, f32[96,128]{1,0:T(8,128)S(1)}, u32[]{:S(2)}, u32[]{:S(2)}) collective-permute-start(f32[96,128]{1,0:T(8,128)S(1)} %get-tuple-element.85), channel_id=1, source_target_pairs={{0,1},{1,0},{2,6},{3,7},{4,5},{5,4},{6,2},{7,3},{8,9},{9,8},{10,14... | collective-permute-start | bytes 147464 | tf_op jit(solution)/shard_map/ppermute | solution.py:748
  17.1 0.0 collective-permute-start.4
  17.1 2.2 %own_back.1 = (f32[128,256]{1,0:T(8,128)S(1)}, f32[16,128]{1,0:T(8,128)S(1)}, f32[1,256]{1,0:T(1,128)S(1)}) custom-call(bf16[2,1024,1152]{2,1,0:T(8,128)(2,1)S(1)} %get-tuple-element.60.group_factor_ref, bf16[2,512,1152]{2,1,0:T(8,128)(2,1)S(1)} %get-tuple-element.61.cell_factor_ref, bf16[2,128,1152]{2,1,0:T(8,128)(2,1)S(1)} %get-tuple-element.77.grad_messages_ref, ...), custom_call_target="tpu_custom_call" | custom-call | flops 905969664 | bytes 8154656 | tf_op jit(solution)/shard_map/own_back/pallas_call | solution.py:593
  19.3 0.4 %collective-permute-done.3.received_ref = f32[96,128]{1,0:T(8,128)S(1)} collective-permute-done((f32[96,128]{1,0:T(8,128)S(1)}, f32[96,128]{1,0:T(8,128)S(1)}, u32[]{:S(2)}, u32[]{:S(2)}) %collective-permute-start.3) | collective-permute-done | bytes 49184 | tf_op jit(solution)/shard_map/ppermute | solution.py:748
  19.7 0.0 collective-permute-done.4.from_pair_ref
  19.7 2.6 %collective-permute-start.7 = (f32[112,128]{1,0:T(8,128)S(1)}, f32[112,128]{1,0:T(8,128)S(1)}, u32[]{:S(2)}, u32[]{:S(2)}) collective-permute-start(f32[112,128]{1,0:T(8,128)S(1)} %join.1), channel_id=1, source_target_pairs={{0,12},{1,13},{2,19},{3,18},{4,8},{5,9},{6,23},{7,22},{8,4},{9,5},... | collective-permute-start | bytes 172040 | tf_op jit(solution)/shard_map/ppermute | solution.py:778
  22.3 0.4 %collective-permute-start.6 = (f32[112,128]{1,0:T(8,128)S(1)}, f32[112,128]{1,0:T(8,128)S(1)}, u32[]{:S(2)}, u32[]{:S(2)}) collective-permute-start(f32[112,128]{1,0:T(8,128)S(1)} %join.1), channel_id=1, source_target_pairs={{0,8},{1,9},{2,18},{3,19},{4,12},{5,13},{6,22},{7,23},{8,0},{9,1},... | collective-permute-start | bytes 172040 | tf_op jit(solution)/shard_map/ppermute | solution.py:778
  22.8 0.5 %collective-permute-start.5 = (f32[112,128]{1,0:T(8,128)S(1)}, f32[112,128]{1,0:T(8,128)S(1)}, u32[]{:S(2)}, u32[]{:S(2)}) collective-permute-start(f32[112,128]{1,0:T(8,128)S(1)} %join.1), channel_id=1, source_target_pairs={{0,4},{1,5},{2,3},{3,2},{4,0},{5,1},{6,7},{7,6},{8,12},{9,13},{10,... | collective-permute-start | bytes 172040 | tf_op jit(solution)/shard_map/ppermute | solution.py:778
  23.3 0.7 %collective-permute-start.8 = (f32[128,128]{1,0:T(8,128)S(1)}, f32[128,128]{1,0:T(8,128)S(1)}, u32[]{:S(2)}, u32[]{:S(2)}) collective-permute-start(f32[128,128]{1,0:T(8,128)S(1)} %get-tuple-element.91), channel_id=1, source_target_pairs={{2,4},{4,2},{6,8},{8,6},{10,12},{12,10},{14,16},{16,14},{18,20},{2... | collective-permute-start | bytes 196616 | tf_op jit(solution)/shard_map/ppermute | solution.py:780
  24.0 1.5 %collective-permute-done.7 = f32[112,128]{1,0:T(8,128)S(1)} collective-permute-done((f32[112,128]{1,0:T(8,128)S(1)}, f32[112,128]{1,0:T(8,128)S(1)}, u32[]{:S(2)}, u32[]{:S(2)}) %collective-permute-start.7) | collective-permute-done | bytes 57376 | tf_op jit(solution)/shard_map/ppermute | solution.py:778
  25.5 1.6 %collective-permute-done.6 = f32[112,128]{1,0:T(8,128)S(1)} collective-permute-done((f32[112,128]{1,0:T(8,128)S(1)}, f32[112,128]{1,0:T(8,128)S(1)}, u32[]{:S(2)}, u32[]{:S(2)}) %collective-permute-start.6) | collective-permute-done | bytes 57376 | tf_op jit(solution)/shard_map/ppermute | solution.py:778
  27.1 0.0 collective-permute-done.5
  27.1 3.4 %collective-permute-start.11 = (f32[112,128]{1,0:T(8,128)S(1)}, f32[112,128]{1,0:T(8,128)S(1)}, u32[]{:S(2)}, u32[]{:S(2)}) collective-permute-start(f32[112,128]{1,0:T(8,128)S(1)} %add_add_fusion.mine_ref), channel_id=1, source_target_pairs={{0,17},{1,16},{2,14},{3,15},{4,21},{5,20},{6,10},{7,11},{8,25},{9,... | collective-permute-start | bytes 172040 | tf_op jit(solution)/shard_map/ppermute | solution.py:784
  30.6 0.5 %collective-permute-start.10 = (f32[112,128]{1,0:T(8,128)S(1)}, f32[112,128]{1,0:T(8,128)S(1)}, u32[]{:S(2)}, u32[]{:S(2)}) collective-permute-start(f32[112,128]{1,0:T(8,128)S(1)} %add_add_fusion.mine_ref), channel_id=1, source_target_pairs={{0,1},{1,0},{2,6},{3,7},{4,5},{5,4},{6,2},{7,3},{8,9},{9,8},{10,14... | collective-permute-start | bytes 172040 | tf_op jit(solution)/shard_map/ppermute | solution.py:784
  31.1 0.5 %collective-permute-start.9 = (f32[112,128]{1,0:T(8,128)S(1)}, f32[112,128]{1,0:T(8,128)S(1)}, u32[]{:S(2)}, u32[]{:S(2)}) collective-permute-start(f32[112,128]{1,0:T(8,128)S(1)} %add_add_fusion.mine_ref), channel_id=1, source_target_pairs={{0,16},{1,17},{2,10},{3,11},{4,20},{5,21},{6,14},{7,15},{8,24},{9,... | collective-permute-start | bytes 172040 | tf_op jit(solution)/shard_map/ppermute | solution.py:784
  31.6 0.0 collective-permute-done.8.from_cross_ref
  31.6 1.6 %collective-permute-done.11.both_ref = f32[112,128]{1,0:T(8,128)S(1)} collective-permute-done((f32[112,128]{1,0:T(8,128)S(1)}, f32[112,128]{1,0:T(8,128)S(1)}, u32[]{:S(2)}, u32[]{:S(2)}) %collective-permute-start.11) | collective-permute-done | bytes 57376 | tf_op jit(solution)/shard_map/ppermute | solution.py:784
  33.2 1.5 %collective-permute-done.10.other_ref = f32[112,128]{1,0:T(8,128)S(1)} collective-permute-done((f32[112,128]{1,0:T(8,128)S(1)}, f32[112,128]{1,0:T(8,128)S(1)}, u32[]{:S(2)}, u32[]{:S(2)}) %collective-permute-start.10) | collective-permute-done | bytes 57376 | tf_op jit(solution)/shard_map/ppermute | solution.py:784
  34.7 2.0 %collective-permute-done.9.along_ref = f32[112,128]{1,0:T(8,128)S(1)} collective-permute-done((f32[112,128]{1,0:T(8,128)S(1)}, f32[112,128]{1,0:T(8,128)S(1)}, u32[]{:S(2)}, u32[]{:S(2)}) %collective-permute-start.9) | collective-permute-done | bytes 57376 | tf_op jit(solution)/shard_map/ppermute | solution.py:784
  36.8 0.1 collective-permute-start.12
  36.9 0.7 %fold.1 = (f32[1,128,256]{2,1,0:T(8,128)}, f32[1,256]{1,0:T(1,128)}) custom-call(f32[128,256]{1,0:T(8,128)S(1)} %get-tuple-element.83.own_ref, f32[128,128]{1,0:T(8,128)S(1)} %collective-permute-done.4.from_pair_ref, f32[128,128]{1,0:T(8,128)S(1)} %collective-permute-done.8.from_cross_ref, f32[1,256]{1,0:T(1,128)S(1)} %get-tuple-element.93.energy_in_ref), custom_call_target="tpu_custom_call" | custom-call | bytes 395264 | tf_op jit(solution)/shard_map/fold/pallas_call | solution.py:593
  37.6 0.6 %collective-permute-done.12.other_ref = f32[208,128]{1,0:T(8,128)S(1)} collective-permute-done((f32[208,128]{1,0:T(8,128)S(1)}, f32[208,128]{1,0:T(8,128)S(1)}, u32[]{:S(2)}, u32[]{:S(2)}) %collective-permute-start.12) | collective-permute-done | bytes 106528 | tf_op jit(solution)/shard_map/ppermute | solution.py:801
  38.2 0.7 %finish.1 = (f32[8,128]{1,0:T(8,128)}, f32[384,128]{1,0:T(8,128)}, f32[1,128]{1,0:T(1,128)}, f32[1,8]{1,0:T(1,128)}) custom-call(f32[208,128]{1,0:T(8,128)S(1)} %gather.1.mine_ref, f32[208,128]{1,0:T(8,128)S(1)} %collective-permute-done.12.other_ref), custom_call_target="tpu_custom_call" | custom-call | bytes 414240 | tf_op jit(solution)/shard_map/finish/pallas_call | solution.py:593
  (4 shorter events, 0.1 us)
Async XLA Ops:
  1.6 5.3 %collective-permute-start = (f32[136,128]{1,0:T(8,128)S(1)}, f32[136,128]{1,0:T(8,128)S(1)}, u32[]{:S(2)}, u32[]{:S(2)}) collective-permute-start(f32[136,128]{1,0:T(8,128)S(1)} %get-tuple-element.58.refs_4_.near_ref), channel_id=1, source_target_pairs={{0,2},{2,0},{4,6},{6,4},{8,10},{10,8},{12,14},{14,12},{16,18},{18,... | collective-permute-start | bytes 208904 | tf_op jit(solution)/shard_map/ppermute | solution.py:658
  2.1 4.8 %collective-permute-start.1 = (f32[136,128]{1,0:T(8,128)S(1)}, f32[136,128]{1,0:T(8,128)S(1)}, u32[]{:S(2)}, u32[]{:S(2)}) collective-permute-start(f32[136,128]{1,0:T(8,128)S(1)} %get-tuple-element.59.refs_5_.far_ref), channel_id=1, source_target_pairs={{2,4},{4,2},{6,8},{8,6},{10,12},{12,10},{14,16},{16,14},{18,20},{2... | collective-permute-start | bytes 208904 | tf_op jit(solution)/shard_map/ppermute | solution.py:657
  10.0 5.5 %collective-permute-start.2 = (f32[192,128]{1,0:T(8,128)S(1)}, f32[192,128]{1,0:T(8,128)S(1)}, u32[]{:S(2)}, u32[]{:S(2)}) collective-permute-start(f32[192,128]{1,0:T(8,128)S(1)} %get-tuple-element.69), channel_id=1, source_target_pairs={{0,2},{2,0},{4,6},{6,4},{8,10},{10,8},{12,14},{14,12},{16,18},{18,... | collective-permute-start | bytes 294920 | tf_op jit(solution)/shard_map/ppermute | solution.py:719
  15.6 4.2 %collective-permute-start.3 = (f32[96,128]{1,0:T(8,128)S(1)}, f32[96,128]{1,0:T(8,128)S(1)}, u32[]{:S(2)}, u32[]{:S(2)}) collective-permute-start(f32[96,128]{1,0:T(8,128)S(1)} %get-tuple-element.85), channel_id=1, source_target_pairs={{0,1},{1,0},{2,6},{3,7},{4,5},{5,4},{6,2},{7,3},{8,9},{9,8},{10,14... | collective-permute-start | bytes 147464 | tf_op jit(solution)/shard_map/ppermute | solution.py:748
  17.1 2.6 %collective-permute-start.4 = (f32[128,128]{1,0:T(8,128)S(1)}, f32[128,128]{1,0:T(8,128)S(1)}, u32[]{:S(2)}, u32[]{:S(2)}) collective-permute-start(f32[128,128]{1,0:T(8,128)S(1)} %get-tuple-element.87), channel_id=1, source_target_pairs={{0,2},{2,0},{4,6},{6,4},{8,10},{10,8},{12,14},{14,12},{16,18},{18,... | collective-permute-start | bytes 196616 | tf_op jit(solution)/shard_map/ppermute | solution.py:749
  19.7 5.8 %collective-permute-start.7 = (f32[112,128]{1,0:T(8,128)S(1)}, f32[112,128]{1,0:T(8,128)S(1)}, u32[]{:S(2)}, u32[]{:S(2)}) collective-permute-start(f32[112,128]{1,0:T(8,128)S(1)} %join.1), channel_id=1, source_target_pairs={{0,12},{1,13},{2,19},{3,18},{4,8},{5,9},{6,23},{7,22},{8,4},{9,5},... | collective-permute-start | bytes 172040 | tf_op jit(solution)/shard_map/ppermute | solution.py:778
  22.3 4.8 %collective-permute-start.6 = (f32[112,128]{1,0:T(8,128)S(1)}, f32[112,128]{1,0:T(8,128)S(1)}, u32[]{:S(2)}, u32[]{:S(2)}) collective-permute-start(f32[112,128]{1,0:T(8,128)S(1)} %join.1), channel_id=1, source_target_pairs={{0,8},{1,9},{2,18},{3,19},{4,12},{5,13},{6,22},{7,23},{8,0},{9,1},... | collective-permute-start | bytes 172040 | tf_op jit(solution)/shard_map/ppermute | solution.py:778
  22.8 4.3 %collective-permute-start.5 = (f32[112,128]{1,0:T(8,128)S(1)}, f32[112,128]{1,0:T(8,128)S(1)}, u32[]{:S(2)}, u32[]{:S(2)}) collective-permute-start(f32[112,128]{1,0:T(8,128)S(1)} %join.1), channel_id=1, source_target_pairs={{0,4},{1,5},{2,3},{3,2},{4,0},{5,1},{6,7},{7,6},{8,12},{9,13},{10,... | collective-permute-start | bytes 172040 | tf_op jit(solution)/shard_map/ppermute | solution.py:778
  23.3 8.3 %collective-permute-start.8 = (f32[128,128]{1,0:T(8,128)S(1)}, f32[128,128]{1,0:T(8,128)S(1)}, u32[]{:S(2)}, u32[]{:S(2)}) collective-permute-start(f32[128,128]{1,0:T(8,128)S(1)} %get-tuple-element.91), channel_id=1, source_target_pairs={{2,4},{4,2},{6,8},{8,6},{10,12},{12,10},{14,16},{16,14},{18,20},{2... | collective-permute-start | bytes 196616 | tf_op jit(solution)/shard_map/ppermute | solution.py:780
  27.1 6.1 %collective-permute-start.11 = (f32[112,128]{1,0:T(8,128)S(1)}, f32[112,128]{1,0:T(8,128)S(1)}, u32[]{:S(2)}, u32[]{:S(2)}) collective-permute-start(f32[112,128]{1,0:T(8,128)S(1)} %add_add_fusion.mine_ref), channel_id=1, source_target_pairs={{0,17},{1,16},{2,14},{3,15},{4,21},{5,20},{6,10},{7,11},{8,25},{9,... | collective-permute-start | bytes 172040 | tf_op jit(solution)/shard_map/ppermute | solution.py:784
  30.6 4.2 %collective-permute-start.10 = (f32[112,128]{1,0:T(8,128)S(1)}, f32[112,128]{1,0:T(8,128)S(1)}, u32[]{:S(2)}, u32[]{:S(2)}) collective-permute-start(f32[112,128]{1,0:T(8,128)S(1)} %add_add_fusion.mine_ref), channel_id=1, source_target_pairs={{0,1},{1,0},{2,6},{3,7},{4,5},{5,4},{6,2},{7,3},{8,9},{9,8},{10,14... | collective-permute-start | bytes 172040 | tf_op jit(solution)/shard_map/ppermute | solution.py:784
  31.1 5.7 %collective-permute-start.9 = (f32[112,128]{1,0:T(8,128)S(1)}, f32[112,128]{1,0:T(8,128)S(1)}, u32[]{:S(2)}, u32[]{:S(2)}) collective-permute-start(f32[112,128]{1,0:T(8,128)S(1)} %add_add_fusion.mine_ref), channel_id=1, source_target_pairs={{0,16},{1,17},{2,10},{3,11},{4,20},{5,21},{6,14},{7,15},{8,24},{9,... | collective-permute-start | bytes 172040 | tf_op jit(solution)/shard_map/ppermute | solution.py:784
  36.8 1.4 %collective-permute-start.12 = (f32[208,128]{1,0:T(8,128)S(1)}, f32[208,128]{1,0:T(8,128)S(1)}, u32[]{:S(2)}, u32[]{:S(2)}) collective-permute-start(f32[208,128]{1,0:T(8,128)S(1)} %gather.1.mine_ref), channel_id=1, source_target_pairs={{0,2},{2,0},{4,6},{6,4},{8,10},{10,8},{12,14},{14,12},{16,18},{18,... | collective-permute-start | bytes 319496 | tf_op jit(solution)/shard_map/ppermute | solution.py:801

commit v2 on v1

--- a/solution.py
+++ b/solution.py
@@ -23,14 +23,13 @@
 message_scale = 0.25
 
 COS_COEFFS = (
-    0.9999999998846169,
-    -4.934802185771876,
-    4.058711815779763,
-    -1.3352602773967561,
-    0.23532080049888648,
-    -0.025785772074137014,
-    0.0019043022864480008,
-    -8.868331860867329e-05,
+    0.9999999889445765,
+    -4.93480111664404,
+    4.058694745521682,
+    -1.3351580223048074,
+    0.2350290226247885,
+    -0.025358285754444005,
+    0.0015936782135993002,
 )
 SINC_COEFFS = (
     0.9999999992502204,
@@ -561,7 +560,7 @@
     across = [(1 << k, 0) for k in range(1, space.bit_length() - 1)]
     shared = (along[0], across[0])
     orders = (across + along[1:], along[:1] + across[1:] + along[1:])
-    orders = (orders[0], orders[1][:-2] + orders[1][:-3:-1])
+    orders = tuple(order[:-2] + order[:-3:-1] for order in orders)
     count = len(orders[0])
 
     def route(*places):

time: 39.1 us -> 37.5 us (0.959)
  waiting for transfers between devices: 9.39 us -> 7.77 us
    ppermute x3, waiting for transfers between devices: 5.19 us -> 2.55 us  [body(): arrived = [lax.ppermute(value, everyone, route) for route in last]]
    ppermute x3, waiting for transfers between devices: 3.16 us -> 4.18 us  [body(): arrived = [lax.ppermute(value, everyone, route) for route in routes]]
    ppermute x3, starting transfers between devices: 4.45 us -> 3.55 us  [body(): arrived = [lax.ppermute(value, everyone, route) for route in last]]
    ppermute x3, starting transfers between devices: 3.55 us -> 4.45 us  [body(): arrived = [lax.ppermute(value, everyone, route) for route in routes]]
  transfers between devices with their start and end apart: 13 -> 13, of which waited for: 7 -> 7; matrix products, arithmetic and copies ran while one was open for 0% -> 0% of each run, Pallas kernels for 20% -> 21%
where the time goes in v2:
time: 37.5 us; the launch traced here: 37.3 us
  starting transfers between devices  15.4 us (41%)
  Pallas kernels  12.7 us (34%)
  waiting for transfers between devices  7.77 us (21%)
  between operations  1.4 us (4%)
    pallas_call x8, Pallas kernels, call(): pl.pallas_call(kernel, out_shape=shapes, in_specs=[vmem] * len(inputs), o...  8.26 us
    ppermute x3, starting transfers between devices, body(): arrived = [lax.ppermute(value, everyone, route) for route in routes]  4.45 us
    ppermute x3, waiting for transfers between devices, body(): arrived = [lax.ppermute(value, everyone, route) for route in routes]  4.18 us
    ppermute x1, starting transfers between devices, body(): received = lax.ppermute(sent, 'space', pair)  3.96 us
    ppermute x3, starting transfers between devices, body(): arrived = [lax.ppermute(value, everyone, route) for route in last]  3.55 us
    pallas_call x1, Pallas kernels, body(): pl.pallas_call(local_kernel, out_shape=(jax.ShapeDtypeStruct((2, NB * GRO...  3.49 us
    ppermute x3, waiting for transfers between devices, body(): arrived = [lax.ppermute(value, everyone, route) for route in last]  2.55 us
    ppermute x1, starting transfers between devices, body(): received = lax.ppermute(sent, everyone, sharing)  1.55 us
  transfers between devices with their start and end apart: 13, of which 7 were waited for; matrix products, arithmetic and copies ran while one was open for 0% of the time, Pallas kernels for 21%

profile of v2, /device:TPU:0, one launch (start us, length us, event | category | flops | bytes accessed | tf_op | source)
XLA Modules:
  0.0 37.3 jit_solution(9891280125421869761)
XLA Ops:
  0.6 0.9 %split.1 = (f32[136,128]{1,0:T(8,128)S(1)}, f32[136,128]{1,0:T(8,128)S(1)}, s32[1,20]{1,0:T(1,128)S(1)}, s32[1,20]{1,0:T(1,128)S(1)}, f32[8,128]{1,0:T(8,128)S(1)}) custom-call(f32[1,128,256]{2,1,0:T(8,128)} %refs_0_.2, f32[3,1,256]{2,1,0:T(1,128)} %bitcast.5, s32[1,20]{1,0:T(1,128)} %refs_2_.1, s32[1,20]{1,0:T(1,128)} %refs_3_.1, f32[8,128]{1,0:T(8,128)} %refs_4_.1), custom_call_target="tpu_custom_call" | custom-call | tf_op jit(solution)/shard_map/split/pallas_call | solution.py:638
  1.6 0.5 %collective-permute-start = (f32[136,128]{1,0:T(8,128)S(1)}, f32[136,128]{1,0:T(8,128)S(1)}, u32[]{:S(2)}, u32[]{:S(2)}) collective-permute-start(f32[136,128]{1,0:T(8,128)S(1)} %get-tuple-element.58.refs_4_.near_ref), channel_id=1, source_target_pairs={{0,2},{2,0},{4,6},{6,4},{8,10},{10,8},{12,14},{14,12},{16,18},{18,... | collective-permute-start | bytes 208904 | tf_op jit(solution)/shard_map/ppermute | solution.py:657
  2.1 0.7 %collective-permute-start.1 = (f32[136,128]{1,0:T(8,128)S(1)}, f32[136,128]{1,0:T(8,128)S(1)}, u32[]{:S(2)}, u32[]{:S(2)}) collective-permute-start(f32[136,128]{1,0:T(8,128)S(1)} %get-tuple-element.59.refs_5_.far_ref), channel_id=1, source_target_pairs={{2,4},{4,2},{6,8},{8,6},{10,12},{12,10},{14,16},{16,14},{18,20},{2... | collective-permute-start | bytes 208904 | tf_op jit(solution)/shard_map/ppermute | solution.py:656
  3.4 3.5 %local_pairs.1 = (bf16[2,1024,1152]{2,1,0:T(8,128)(2,1)S(1)}, bf16[2,512,1152]{2,1,0:T(8,128)(2,1)S(1)}, f32[2,128,1152]{2,1,0:T(8,128)S(1)}, f32[8,128]{1,0:T(8...) custom-call(s32[1,1]{1,0:T(1,128)S(6)} %copy.17.refs_0_, ...), custom_call_target="tpu_custom_call" | custom-call | flops 905969664 | bytes 11000000 | tf_op jit(solution)/shard_map/local_pairs/pallas_call | solution.py:660
  6.9 0.0 collective-permute-done.from_pair_ref
  6.9 0.0 collective-permute-done.1.from_cross_ref
  6.9 3.1 %node_stage.1 = (f32[128,256]{1,0:T(8,128)S(1)}, f32[192,128]{1,0:T(8,128)S(1)}, f32[192,128]{1,0:T(8,128)S(1)}, bf16[2,128,1152]{2,1,0:T(8,128)(2,1)S(1)}, bf16...) custom-call(f32[136,128]{1,0:T(8,128)S(1)} %get-tuple-element.58.refs_4_.near_ref, ...), custom_call_target="tpu_custom_call" | custom-call | flops 603979776 | bytes 7595520 | tf_op jit(solution)/shard_map/node_stage/pallas_call | solution.py:592
  10.0 4.0 %collective-permute-start.2 = (f32[192,128]{1,0:T(8,128)S(1)}, f32[192,128]{1,0:T(8,128)S(1)}, u32[]{:S(2)}, u32[]{:S(2)}) collective-permute-start(f32[192,128]{1,0:T(8,128)S(1)} %get-tuple-element.69), channel_id=1, source_target_pairs={{0,2},{2,0},{4,6},{6,4},{8,10},{10,8},{12,14},{14,12},{16,18},{18,... | collective-permute-start | bytes 294920 | tf_op jit(solution)/shard_map/ppermute | solution.py:718
  14.0 1.6 %halo_back.1 = (f32[128,128]{1,0:T(8,128)S(1)}, f32[128,128]{1,0:T(8,128)S(1)}, f32[128,128]{1,0:T(8,128)S(1)}, f32[8,128]{1,0:T(8,128)S(1)}) custom-call(bf16[2,512,1152]{2,1,0:T(8,128)(2,1)S(1)} %get-tuple-element.70.cell_factor_ref, bf16[2,512,1152]{2,1,0:T(8,128)(2,1)S(1)} %get-tuple-element.71.merged_factor_ref, ...), custom_call_target="tpu_custom_call" | custom-call | flops 603979776 | bytes 5791744 | tf_op jit(solution)/shard_map/halo_back/pallas_call | solution.py:592
  15.5 0.0 collective-permute-done.2.received_ref
  15.6 1.6 %collective-permute-start.3 = (f32[96,128]{1,0:T(8,128)S(1)}, f32[96,128]{1,0:T(8,128)S(1)}, u32[]{:S(2)}, u32[]{:S(2)}) collective-permute-start(f32[96,128]{1,0:T(8,128)S(1)} %get-tuple-element.85), channel_id=1, source_target_pairs={{0,1},{1,0},{2,6},{3,7},{4,5},{5,4},{6,2},{7,3},{8,9},{9,8},{10,14... | collective-permute-start | bytes 147464 | tf_op jit(solution)/shard_map/ppermute | solution.py:747
  17.1 0.0 collective-permute-start.4
  17.1 2.2 %own_back.1 = (f32[128,256]{1,0:T(8,128)S(1)}, f32[16,128]{1,0:T(8,128)S(1)}, f32[1,256]{1,0:T(1,128)S(1)}) custom-call(bf16[2,1024,1152]{2,1,0:T(8,128)(2,1)S(1)} %get-tuple-element.60.group_factor_ref, bf16[2,512,1152]{2,1,0:T(8,128)(2,1)S(1)} %get-tuple-element.61.cell_factor_ref, bf16[2,128,1152]{2,1,0:T(8,128)(2,1)S(1)} %get-tuple-element.77.grad_messages_ref, ...), custom_call_target="tpu_custom_call" | custom-call | flops 905969664 | bytes 8154656 | tf_op jit(solution)/shard_map/own_back/pallas_call | solution.py:592
  19.3 0.4 %collective-permute-done.3.received_ref = f32[96,128]{1,0:T(8,128)S(1)} collective-permute-done((f32[96,128]{1,0:T(8,128)S(1)}, f32[96,128]{1,0:T(8,128)S(1)}, u32[]{:S(2)}, u32[]{:S(2)}) %collective-permute-start.3) | collective-permute-done | bytes 49184 | tf_op jit(solution)/shard_map/ppermute | solution.py:747
  19.8 0.0 collective-permute-done.4.from_pair_ref
  19.8 3.6 %collective-permute-start.7 = (f32[112,128]{1,0:T(8,128)S(1)}, f32[112,128]{1,0:T(8,128)S(1)}, u32[]{:S(2)}, u32[]{:S(2)}) collective-permute-start(f32[112,128]{1,0:T(8,128)S(1)} %join.1), channel_id=1, source_target_pairs={{0,20},{1,21},{2,19},{3,18},{4,16},{5,17},{6,23},{7,22},{8,28},{9,... | collective-permute-start | bytes 172040 | tf_op jit(solution)/shard_map/ppermute | solution.py:777
  23.4 0.3 collective-permute-start.6
  23.7 0.5 %collective-permute-start.5 = (f32[112,128]{1,0:T(8,128)S(1)}, f32[112,128]{1,0:T(8,128)S(1)}, u32[]{:S(2)}, u32[]{:S(2)}) collective-permute-start(f32[112,128]{1,0:T(8,128)S(1)} %join.1), channel_id=1, source_target_pairs={{0,4},{1,5},{2,3},{3,2},{4,0},{5,1},{6,7},{7,6},{8,12},{9,13},{10,... | collective-permute-start | bytes 172040 | tf_op jit(solution)/shard_map/ppermute | solution.py:777
  24.2 0.7 %collective-permute-start.8 = (f32[128,128]{1,0:T(8,128)S(1)}, f32[128,128]{1,0:T(8,128)S(1)}, u32[]{:S(2)}, u32[]{:S(2)}) collective-permute-start(f32[128,128]{1,0:T(8,128)S(1)} %get-tuple-element.91), channel_id=1, source_target_pairs={{2,4},{4,2},{6,8},{8,6},{10,12},{12,10},{14,16},{16,14},{18,20},{2... | collective-permute-start | bytes 196616 | tf_op jit(solution)/shard_map/ppermute | solution.py:779
  24.9 2.3 %collective-permute-done.7 = f32[112,128]{1,0:T(8,128)S(1)} collective-permute-done((f32[112,128]{1,0:T(8,128)S(1)}, f32[112,128]{1,0:T(8,128)S(1)}, u32[]{:S(2)}, u32[]{:S(2)}) %collective-permute-start.7) | collective-permute-done | bytes 57376 | tf_op jit(solution)/shard_map/ppermute | solution.py:777
  27.2 1.9 %collective-permute-done.6 = f32[112,128]{1,0:T(8,128)S(1)} collective-permute-done((f32[112,128]{1,0:T(8,128)S(1)}, f32[112,128]{1,0:T(8,128)S(1)}, u32[]{:S(2)}, u32[]{:S(2)}) %collective-permute-start.6) | collective-permute-done | bytes 57376 | tf_op jit(solution)/shard_map/ppermute | solution.py:777
  29.1 0.0 collective-permute-done.5
  29.1 1.4 %collective-permute-start.11 = (f32[112,128]{1,0:T(8,128)S(1)}, f32[112,128]{1,0:T(8,128)S(1)}, u32[]{:S(2)}, u32[]{:S(2)}) collective-permute-start(f32[112,128]{1,0:T(8,128)S(1)} %add_add_fusion.mine_ref), channel_id=1, source_target_pairs={{0,9},{1,8},{2,14},{3,15},{4,13},{5,12},{6,10},{7,11},{8,1},{9,0},... | collective-permute-start | bytes 172040 | tf_op jit(solution)/shard_map/ppermute | solution.py:783
  30.5 0.5 %collective-permute-start.10 = (f32[112,128]{1,0:T(8,128)S(1)}, f32[112,128]{1,0:T(8,128)S(1)}, u32[]{:S(2)}, u32[]{:S(2)}) collective-permute-start(f32[112,128]{1,0:T(8,128)S(1)} %add_add_fusion.mine_ref), channel_id=1, source_target_pairs={{0,1},{1,0},{2,6},{3,7},{4,5},{5,4},{6,2},{7,3},{8,9},{9,8},{10,14... | collective-permute-start | bytes 172040 | tf_op jit(solution)/shard_map/ppermute | solution.py:783
  31.0 1.6 %collective-permute-start.9 = (f32[112,128]{1,0:T(8,128)S(1)}, f32[112,128]{1,0:T(8,128)S(1)}, u32[]{:S(2)}, u32[]{:S(2)}) collective-permute-start(f32[112,128]{1,0:T(8,128)S(1)} %add_add_fusion.mine_ref), channel_id=1, source_target_pairs={{0,8},{1,9},{2,10},{3,11},{4,12},{5,13},{6,14},{7,15},{8,0},{9,1},... | collective-permute-start | bytes 172040 | tf_op jit(solution)/shard_map/ppermute | solution.py:783
  32.6 0.0 collective-permute-done.8.from_cross_ref
  32.6 1.9 %collective-permute-done.11.both_ref = f32[112,128]{1,0:T(8,128)S(1)} collective-permute-done((f32[112,128]{1,0:T(8,128)S(1)}, f32[112,128]{1,0:T(8,128)S(1)}, u32[]{:S(2)}, u32[]{:S(2)}) %collective-permute-start.11) | collective-permute-done | bytes 57376 | tf_op jit(solution)/shard_map/ppermute | solution.py:783
  34.6 0.4 collective-permute-done.10.other_ref
  34.9 0.3 collective-permute-done.9.along_ref
  35.2 0.1 collective-permute-start.12
  35.3 0.7 %fold.1 = (f32[1,128,256]{2,1,0:T(8,128)}, f32[1,256]{1,0:T(1,128)}) custom-call(f32[128,256]{1,0:T(8,128)S(1)} %get-tuple-element.83.own_ref, f32[128,128]{1,0:T(8,128)S(1)} %collective-permute-done.4.from_pair_ref, f32[128,128]{1,0:T(8,128)S(1)} %collective-permute-done.8.from_cross_ref, f32[1,256]{1,0:T(1,128)S(1)} %get-tuple-element.93.energy_in_ref), custom_call_target="tpu_custom_call" | custom-call | bytes 395264 | tf_op jit(solution)/shard_map/fold/pallas_call | solution.py:592
  36.0 0.6 %collective-permute-done.12.other_ref = f32[208,128]{1,0:T(8,128)S(1)} collective-permute-done((f32[208,128]{1,0:T(8,128)S(1)}, f32[208,128]{1,0:T(8,128)S(1)}, u32[]{:S(2)}, u32[]{:S(2)}) %collective-permute-start.12) | collective-permute-done | bytes 106528 | tf_op jit(solution)/shard_map/ppermute | solution.py:800
  36.6 0.7 %finish.1 = (f32[8,128]{1,0:T(8,128)}, f32[384,128]{1,0:T(8,128)}, f32[1,128]{1,0:T(1,128)}, f32[1,8]{1,0:T(1,128)}) custom-call(f32[208,128]{1,0:T(8,128)S(1)} %gather.1.mine_ref, f32[208,128]{1,0:T(8,128)S(1)} %collective-permute-done.12.other_ref), custom_call_target="tpu_custom_call" | custom-call | bytes 414240 | tf_op jit(solution)/shard_map/finish/pallas_call | solution.py:592
  (4 shorter events, 0.1 us)
Async XLA Ops:
  1.6 5.3 %collective-permute-start = (f32[136,128]{1,0:T(8,128)S(1)}, f32[136,128]{1,0:T(8,128)S(1)}, u32[]{:S(2)}, u32[]{:S(2)}) collective-permute-start(f32[136,128]{1,0:T(8,128)S(1)} %get-tuple-element.58.refs_4_.near_ref), channel_id=1, source_target_pairs={{0,2},{2,0},{4,6},{6,4},{8,10},{10,8},{12,14},{14,12},{16,18},{18,... | collective-permute-start | bytes 208904 | tf_op jit(solution)/shard_map/ppermute | solution.py:657
  2.1 4.8 %collective-permute-start.1 = (f32[136,128]{1,0:T(8,128)S(1)}, f32[136,128]{1,0:T(8,128)S(1)}, u32[]{:S(2)}, u32[]{:S(2)}) collective-permute-start(f32[136,128]{1,0:T(8,128)S(1)} %get-tuple-element.59.refs_5_.far_ref), channel_id=1, source_target_pairs={{2,4},{4,2},{6,8},{8,6},{10,12},{12,10},{14,16},{16,14},{18,20},{2... | collective-permute-start | bytes 208904 | tf_op jit(solution)/shard_map/ppermute | solution.py:656
  10.0 5.5 %collective-permute-start.2 = (f32[192,128]{1,0:T(8,128)S(1)}, f32[192,128]{1,0:T(8,128)S(1)}, u32[]{:S(2)}, u32[]{:S(2)}) collective-permute-start(f32[192,128]{1,0:T(8,128)S(1)} %get-tuple-element.69), channel_id=1, source_target_pairs={{0,2},{2,0},{4,6},{6,4},{8,10},{10,8},{12,14},{14,12},{16,18},{18,... | collective-permute-start | bytes 294920 | tf_op jit(solution)/shard_map/ppermute | solution.py:718
  15.6 4.2 %collective-permute-start.3 = (f32[96,128]{1,0:T(8,128)S(1)}, f32[96,128]{1,0:T(8,128)S(1)}, u32[]{:S(2)}, u32[]{:S(2)}) collective-permute-start(f32[96,128]{1,0:T(8,128)S(1)} %get-tuple-element.85), channel_id=1, source_target_pairs={{0,1},{1,0},{2,6},{3,7},{4,5},{5,4},{6,2},{7,3},{8,9},{9,8},{10,14... | collective-permute-start | bytes 147464 | tf_op jit(solution)/shard_map/ppermute | solution.py:747
  17.1 2.6 %collective-permute-start.4 = (f32[128,128]{1,0:T(8,128)S(1)}, f32[128,128]{1,0:T(8,128)S(1)}, u32[]{:S(2)}, u32[]{:S(2)}) collective-permute-start(f32[128,128]{1,0:T(8,128)S(1)} %get-tuple-element.87), channel_id=1, source_target_pairs={{0,2},{2,0},{4,6},{6,4},{8,10},{10,8},{12,14},{14,12},{16,18},{18,... | collective-permute-start | bytes 196616 | tf_op jit(solution)/shard_map/ppermute | solution.py:748
  19.8 7.4 %collective-permute-start.7 = (f32[112,128]{1,0:T(8,128)S(1)}, f32[112,128]{1,0:T(8,128)S(1)}, u32[]{:S(2)}, u32[]{:S(2)}) collective-permute-start(f32[112,128]{1,0:T(8,128)S(1)} %join.1), channel_id=1, source_target_pairs={{0,20},{1,21},{2,19},{3,18},{4,16},{5,17},{6,23},{7,22},{8,28},{9,... | collective-permute-start | bytes 172040 | tf_op jit(solution)/shard_map/ppermute | solution.py:777
  23.4 5.7 %collective-permute-start.6 = (f32[112,128]{1,0:T(8,128)S(1)}, f32[112,128]{1,0:T(8,128)S(1)}, u32[]{:S(2)}, u32[]{:S(2)}) collective-permute-start(f32[112,128]{1,0:T(8,128)S(1)} %join.1), channel_id=1, source_target_pairs={{0,16},{1,17},{2,18},{3,19},{4,20},{5,21},{6,22},{7,23},{8,24},{9,... | collective-permute-start | bytes 172040 | tf_op jit(solution)/shard_map/ppermute | solution.py:777
  23.7 5.3 %collective-permute-start.5 = (f32[112,128]{1,0:T(8,128)S(1)}, f32[112,128]{1,0:T(8,128)S(1)}, u32[]{:S(2)}, u32[]{:S(2)}) collective-permute-start(f32[112,128]{1,0:T(8,128)S(1)} %join.1), channel_id=1, source_target_pairs={{0,4},{1,5},{2,3},{3,2},{4,0},{5,1},{6,7},{7,6},{8,12},{9,13},{10,... | collective-permute-start | bytes 172040 | tf_op jit(solution)/shard_map/ppermute | solution.py:777
  24.2 8.4 %collective-permute-start.8 = (f32[128,128]{1,0:T(8,128)S(1)}, f32[128,128]{1,0:T(8,128)S(1)}, u32[]{:S(2)}, u32[]{:S(2)}) collective-permute-start(f32[128,128]{1,0:T(8,128)S(1)} %get-tuple-element.91), channel_id=1, source_target_pairs={{2,4},{4,2},{6,8},{8,6},{10,12},{12,10},{14,16},{16,14},{18,20},{2... | collective-permute-start | bytes 196616 | tf_op jit(solution)/shard_map/ppermute | solution.py:779
  29.1 5.5 %collective-permute-start.11 = (f32[112,128]{1,0:T(8,128)S(1)}, f32[112,128]{1,0:T(8,128)S(1)}, u32[]{:S(2)}, u32[]{:S(2)}) collective-permute-start(f32[112,128]{1,0:T(8,128)S(1)} %add_add_fusion.mine_ref), channel_id=1, source_target_pairs={{0,9},{1,8},{2,14},{3,15},{4,13},{5,12},{6,10},{7,11},{8,1},{9,0},... | collective-permute-start | bytes 172040 | tf_op jit(solution)/shard_map/ppermute | solution.py:783
  30.5 4.4 %collective-permute-start.10 = (f32[112,128]{1,0:T(8,128)S(1)}, f32[112,128]{1,0:T(8,128)S(1)}, u32[]{:S(2)}, u32[]{:S(2)}) collective-permute-start(f32[112,128]{1,0:T(8,128)S(1)} %add_add_fusion.mine_ref), channel_id=1, source_target_pairs={{0,1},{1,0},{2,6},{3,7},{4,5},{5,4},{6,2},{7,3},{8,9},{9,8},{10,14... | collective-permute-start | bytes 172040 | tf_op jit(solution)/shard_map/ppermute | solution.py:783
  31.0 4.2 %collective-permute-start.9 = (f32[112,128]{1,0:T(8,128)S(1)}, f32[112,128]{1,0:T(8,128)S(1)}, u32[]{:S(2)}, u32[]{:S(2)}) collective-permute-start(f32[112,128]{1,0:T(8,128)S(1)} %add_add_fusion.mine_ref), channel_id=1, source_target_pairs={{0,8},{1,9},{2,10},{3,11},{4,12},{5,13},{6,14},{7,15},{8,0},{9,1},... | collective-permute-start | bytes 172040 | tf_op jit(solution)/shard_map/ppermute | solution.py:783
  35.2 1.4 %collective-permute-start.12 = (f32[208,128]{1,0:T(8,128)S(1)}, f32[208,128]{1,0:T(8,128)S(1)}, u32[]{:S(2)}, u32[]{:S(2)}) collective-permute-start(f32[208,128]{1,0:T(8,128)S(1)} %gather.1.mine_ref), channel_id=1, source_target_pairs={{0,2},{2,0},{4,6},{6,4},{8,10},{10,8},{12,14},{14,12},{16,18},{18,... | collective-permute-start | bytes 319496 | tf_op jit(solution)/shard_map/ppermute | solution.py:800

commit v3 on v2

--- a/solution.py
+++ b/solution.py
@@ -51,11 +51,9 @@
 SLAB_ROWS = CH + 8
 
 
-def polynomial(coeffs, x):
-    total = coeffs[-1] * x + coeffs[-2]
-    for c in coeffs[-3::-1]:
-        total = total * x + c
-    return total
+def polynomial(coeffs, x, x2, x4):
+    low = (coeffs[0] + coeffs[1] * x) + (coeffs[2] + coeffs[3] * x) * x2
+    return low + ((coeffs[4] + coeffs[5] * x) + coeffs[6] * x2) * x4
 
 
 def factor_rows(factor_ref, size, row, source, target, keep):
@@ -66,11 +64,15 @@
     square = xx + yy + zz
     inside = jnp.minimum(square, 1.0)
     gap = 1.0 - inside
-    base = (gap * gap) * keep * polynomial(SINC_COEFFS, inside)
-    twice_cos = polynomial([2.0 * c for c in COS_COEFFS], inside)
+    inside2 = inside * inside
+    inside4 = inside2 * inside2
+    base = (gap * gap) * keep * polynomial(SINC_COEFFS, inside, inside2, inside4)
+    twice_cos = polynomial([2.0 * c for c in COS_COEFFS], inside, inside2, inside4)
+    twice_cos2 = twice_cos * twice_cos - 2.0
     raw = [base, twice_cos * base]
-    for _ in range(NB - 2):
-        raw.append(twice_cos * raw[-1] - raw[-2])
+    raw += [twice_cos2 * base + base, twice_cos2 * raw[1]]
+    for b in range(4, NB):
+        raw.append(twice_cos2 * raw[b - 2] - raw[b - 4])
     radial = [value if b == 0 else value * (1.0 / (b + 1)) for b, value in enumerate(raw)]
     root_three = math.sqrt(3.0)
     root_fifteen = math.sqrt(15.0)

time: 37.5 us -> 37.4 us (level)
  no operation moved by 1% of the time
where the time goes in v3:
time: 37.4 us; the launch traced here: 37.1 us
  starting transfers between devices  15.4 us (41%)
  Pallas kernels  12.5 us (33%)
  waiting for transfers between devices  7.78 us (21%)
  between operations  1.4 us (4%)
    pallas_call x8, Pallas kernels, call(): pl.pallas_call(kernel, out_shape=shapes, in_specs=[vmem] * len(inputs), o...  8.22 us
    ppermute x3, starting transfers between devices, body(): arrived = [lax.ppermute(value, everyone, route) for route in routes]  4.45 us
    ppermute x3, waiting for transfers between devices, body(): arrived = [lax.ppermute(value, everyone, route) for route in routes]  4.18 us
    ppermute x1, starting transfers between devices, body(): received = lax.ppermute(sent, 'space', pair)  3.96 us
    ppermute x3, starting transfers between devices, body(): arrived = [lax.ppermute(value, everyone, route) for route in last]  3.55 us
    pallas_call x1, Pallas kernels, body(): pl.pallas_call(local_kernel, out_shape=(jax.ShapeDtypeStruct((2, NB * GRO...  3.36 us
    ppermute x3, waiting for transfers between devices, body(): arrived = [lax.ppermute(value, everyone, route) for route in last]  2.55 us
    ppermute x1, starting transfers between devices, body(): received = lax.ppermute(sent, everyone, sharing)  1.56 us
  transfers between devices with their start and end apart: 13, of which 7 were waited for; matrix products, arithmetic and copies ran while one was open for 0% of the time, Pallas kernels for 21%

profile of v3, /device:TPU:0, one launch (start us, length us, event | category | flops | bytes accessed | tf_op | source)
XLA Modules:
  0.0 37.1 jit_solution(13832539985736880334)
XLA Ops:
  0.6 0.9 %split.1 = (f32[136,128]{1,0:T(8,128)S(1)}, f32[136,128]{1,0:T(8,128)S(1)}, s32[1,20]{1,0:T(1,128)S(1)}, s32[1,20]{1,0:T(1,128)S(1)}, f32[8,128]{1,0:T(8,128)S(1)}) custom-call(f32[1,128,256]{2,1,0:T(8,128)} %refs_0_.2, f32[3,1,256]{2,1,0:T(1,128)} %bitcast.5, s32[1,20]{1,0:T(1,128)} %refs_2_.1, s32[1,20]{1,0:T(1,128)} %refs_3_.1, f32[8,128]{1,0:T(8,128)} %refs_4_.1), custom_call_target="tpu_custom_call" | custom-call | tf_op jit(solution)/shard_map/split/pallas_call | solution.py:640
  1.6 0.5 %collective-permute-start = (f32[136,128]{1,0:T(8,128)S(1)}, f32[136,128]{1,0:T(8,128)S(1)}, u32[]{:S(2)}, u32[]{:S(2)}) collective-permute-start(f32[136,128]{1,0:T(8,128)S(1)} %get-tuple-element.58.refs_4_.near_ref), channel_id=1, source_target_pairs={{0,2},{2,0},{4,6},{6,4},{8,10},{10,8},{12,14},{14,12},{16,18},{18,... | collective-permute-start | bytes 208904 | tf_op jit(solution)/shard_map/ppermute | solution.py:659
  2.1 0.7 %collective-permute-start.1 = (f32[136,128]{1,0:T(8,128)S(1)}, f32[136,128]{1,0:T(8,128)S(1)}, u32[]{:S(2)}, u32[]{:S(2)}) collective-permute-start(f32[136,128]{1,0:T(8,128)S(1)} %get-tuple-element.59.refs_5_.far_ref), channel_id=1, source_target_pairs={{2,4},{4,2},{6,8},{8,6},{10,12},{12,10},{14,16},{16,14},{18,20},{2... | collective-permute-start | bytes 208904 | tf_op jit(solution)/shard_map/ppermute | solution.py:658
  3.4 3.4 %local_pairs.1 = (bf16[2,1024,1152]{2,1,0:T(8,128)(2,1)S(1)}, bf16[2,512,1152]{2,1,0:T(8,128)(2,1)S(1)}, f32[2,128,1152]{2,1,0:T(8,128)S(1)}, f32[8,128]{1,0:T(8...) custom-call(s32[1,1]{1,0:T(1,128)S(6)} %copy.17.refs_0_, ...), custom_call_target="tpu_custom_call" | custom-call | flops 905969664 | bytes 11000000 | tf_op jit(solution)/shard_map/local_pairs/pallas_call | solution.py:662
  6.8 0.0 collective-permute-done.from_pair_ref
  6.8 0.0 collective-permute-done.1.from_cross_ref
  6.8 3.0 %node_stage.1 = (f32[128,256]{1,0:T(8,128)S(1)}, f32[192,128]{1,0:T(8,128)S(1)}, f32[192,128]{1,0:T(8,128)S(1)}, bf16[2,128,1152]{2,1,0:T(8,128)(2,1)S(1)}, bf16...) custom-call(f32[136,128]{1,0:T(8,128)S(1)} %get-tuple-element.58.refs_4_.near_ref, ...), custom_call_target="tpu_custom_call" | custom-call | flops 603979776 | bytes 7595520 | tf_op jit(solution)/shard_map/node_stage/pallas_call | solution.py:594
  9.8 4.0 %collective-permute-start.2 = (f32[192,128]{1,0:T(8,128)S(1)}, f32[192,128]{1,0:T(8,128)S(1)}, u32[]{:S(2)}, u32[]{:S(2)}) collective-permute-start(f32[192,128]{1,0:T(8,128)S(1)} %get-tuple-element.69), channel_id=1, source_target_pairs={{0,2},{2,0},{4,6},{6,4},{8,10},{10,8},{12,14},{14,12},{16,18},{18,... | collective-permute-start | bytes 294920 | tf_op jit(solution)/shard_map/ppermute | solution.py:720
  13.8 1.6 %halo_back.1 = (f32[128,128]{1,0:T(8,128)S(1)}, f32[128,128]{1,0:T(8,128)S(1)}, f32[128,128]{1,0:T(8,128)S(1)}, f32[8,128]{1,0:T(8,128)S(1)}) custom-call(bf16[2,512,1152]{2,1,0:T(8,128)(2,1)S(1)} %get-tuple-element.70.cell_factor_ref, bf16[2,512,1152]{2,1,0:T(8,128)(2,1)S(1)} %get-tuple-element.71.merged_factor_ref, ...), custom_call_target="tpu_custom_call" | custom-call | flops 603979776 | bytes 5791744 | tf_op jit(solution)/shard_map/halo_back/pallas_call | solution.py:594
  15.4 0.0 collective-permute-done.2.received_ref
  15.4 1.6 %collective-permute-start.3 = (f32[96,128]{1,0:T(8,128)S(1)}, f32[96,128]{1,0:T(8,128)S(1)}, u32[]{:S(2)}, u32[]{:S(2)}) collective-permute-start(f32[96,128]{1,0:T(8,128)S(1)} %get-tuple-element.85), channel_id=1, source_target_pairs={{0,1},{1,0},{2,6},{3,7},{4,5},{5,4},{6,2},{7,3},{8,9},{9,8},{10,14... | collective-permute-start | bytes 147464 | tf_op jit(solution)/shard_map/ppermute | solution.py:749
  17.0 0.0 collective-permute-start.4
  17.0 2.2 %own_back.1 = (f32[128,256]{1,0:T(8,128)S(1)}, f32[16,128]{1,0:T(8,128)S(1)}, f32[1,256]{1,0:T(1,128)S(1)}) custom-call(bf16[2,1024,1152]{2,1,0:T(8,128)(2,1)S(1)} %get-tuple-element.60.group_factor_ref, bf16[2,512,1152]{2,1,0:T(8,128)(2,1)S(1)} %get-tuple-element.61.cell_factor_ref, bf16[2,128,1152]{2,1,0:T(8,128)(2,1)S(1)} %get-tuple-element.77.grad_messages_ref, ...), custom_call_target="tpu_custom_call" | custom-call | flops 905969664 | bytes 8154656 | tf_op jit(solution)/shard_map/own_back/pallas_call | solution.py:594
  19.2 0.4 %collective-permute-done.3.received_ref = f32[96,128]{1,0:T(8,128)S(1)} collective-permute-done((f32[96,128]{1,0:T(8,128)S(1)}, f32[96,128]{1,0:T(8,128)S(1)}, u32[]{:S(2)}, u32[]{:S(2)}) %collective-permute-start.3) | collective-permute-done | bytes 49184 | tf_op jit(solution)/shard_map/ppermute | solution.py:749
  19.6 0.0 collective-permute-done.4.from_pair_ref
  19.6 3.6 %collective-permute-start.7 = (f32[112,128]{1,0:T(8,128)S(1)}, f32[112,128]{1,0:T(8,128)S(1)}, u32[]{:S(2)}, u32[]{:S(2)}) collective-permute-start(f32[112,128]{1,0:T(8,128)S(1)} %join.1), channel_id=1, source_target_pairs={{0,20},{1,21},{2,19},{3,18},{4,16},{5,17},{6,23},{7,22},{8,28},{9,... | collective-permute-start | bytes 172040 | tf_op jit(solution)/shard_map/ppermute | solution.py:779
  23.2 0.3 collective-permute-start.6
  23.6 0.5 %collective-permute-start.5 = (f32[112,128]{1,0:T(8,128)S(1)}, f32[112,128]{1,0:T(8,128)S(1)}, u32[]{:S(2)}, u32[]{:S(2)}) collective-permute-start(f32[112,128]{1,0:T(8,128)S(1)} %join.1), channel_id=1, source_target_pairs={{0,4},{1,5},{2,3},{3,2},{4,0},{5,1},{6,7},{7,6},{8,12},{9,13},{10,... | collective-permute-start | bytes 172040 | tf_op jit(solution)/shard_map/ppermute | solution.py:779
  24.1 0.7 %collective-permute-start.8 = (f32[128,128]{1,0:T(8,128)S(1)}, f32[128,128]{1,0:T(8,128)S(1)}, u32[]{:S(2)}, u32[]{:S(2)}) collective-permute-start(f32[128,128]{1,0:T(8,128)S(1)} %get-tuple-element.91), channel_id=1, source_target_pairs={{2,4},{4,2},{6,8},{8,6},{10,12},{12,10},{14,16},{16,14},{18,20},{2... | collective-permute-start | bytes 196616 | tf_op jit(solution)/shard_map/ppermute | solution.py:781
  24.7 2.3 %collective-permute-done.7 = f32[112,128]{1,0:T(8,128)S(1)} collective-permute-done((f32[112,128]{1,0:T(8,128)S(1)}, f32[112,128]{1,0:T(8,128)S(1)}, u32[]{:S(2)}, u32[]{:S(2)}) %collective-permute-start.7) | collective-permute-done | bytes 57376 | tf_op jit(solution)/shard_map/ppermute | solution.py:779
  27.0 1.9 %collective-permute-done.6 = f32[112,128]{1,0:T(8,128)S(1)} collective-permute-done((f32[112,128]{1,0:T(8,128)S(1)}, f32[112,128]{1,0:T(8,128)S(1)}, u32[]{:S(2)}, u32[]{:S(2)}) %collective-permute-start.6) | collective-permute-done | bytes 57376 | tf_op jit(solution)/shard_map/ppermute | solution.py:779
  28.9 0.0 collective-permute-done.5
  28.9 1.4 %collective-permute-start.11 = (f32[112,128]{1,0:T(8,128)S(1)}, f32[112,128]{1,0:T(8,128)S(1)}, u32[]{:S(2)}, u32[]{:S(2)}) collective-permute-start(f32[112,128]{1,0:T(8,128)S(1)} %add_add_fusion.mine_ref), channel_id=1, source_target_pairs={{0,9},{1,8},{2,14},{3,15},{4,13},{5,12},{6,10},{7,11},{8,1},{9,0},... | collective-permute-start | bytes 172040 | tf_op jit(solution)/shard_map/ppermute | solution.py:785
  30.3 0.5 %collective-permute-start.10 = (f32[112,128]{1,0:T(8,128)S(1)}, f32[112,128]{1,0:T(8,128)S(1)}, u32[]{:S(2)}, u32[]{:S(2)}) collective-permute-start(f32[112,128]{1,0:T(8,128)S(1)} %add_add_fusion.mine_ref), channel_id=1, source_target_pairs={{0,1},{1,0},{2,6},{3,7},{4,5},{5,4},{6,2},{7,3},{8,9},{9,8},{10,14... | collective-permute-start | bytes 172040 | tf_op jit(solution)/shard_map/ppermute | solution.py:785
  30.9 1.6 %collective-permute-start.9 = (f32[112,128]{1,0:T(8,128)S(1)}, f32[112,128]{1,0:T(8,128)S(1)}, u32[]{:S(2)}, u32[]{:S(2)}) collective-permute-start(f32[112,128]{1,0:T(8,128)S(1)} %add_add_fusion.mine_ref), channel_id=1, source_target_pairs={{0,8},{1,9},{2,10},{3,11},{4,12},{5,13},{6,14},{7,15},{8,0},{9,1},... | collective-permute-start | bytes 172040 | tf_op jit(solution)/shard_map/ppermute | solution.py:785
  32.5 0.0 collective-permute-done.8.from_cross_ref
  32.5 1.9 %collective-permute-done.11.both_ref = f32[112,128]{1,0:T(8,128)S(1)} collective-permute-done((f32[112,128]{1,0:T(8,128)S(1)}, f32[112,128]{1,0:T(8,128)S(1)}, u32[]{:S(2)}, u32[]{:S(2)}) %collective-permute-start.11) | collective-permute-done | bytes 57376 | tf_op jit(solution)/shard_map/ppermute | solution.py:785
  34.4 0.4 collective-permute-done.10.other_ref
  34.8 0.3 collective-permute-done.9.along_ref
  35.1 0.1 collective-permute-start.12
  35.1 0.7 %fold.1 = (f32[1,128,256]{2,1,0:T(8,128)}, f32[1,256]{1,0:T(1,128)}) custom-call(f32[128,256]{1,0:T(8,128)S(1)} %get-tuple-element.83.own_ref, f32[128,128]{1,0:T(8,128)S(1)} %collective-permute-done.4.from_pair_ref, f32[128,128]{1,0:T(8,128)S(1)} %collective-permute-done.8.from_cross_ref, f32[1,256]{1,0:T(1,128)S(1)} %get-tuple-element.93.energy_in_ref), custom_call_target="tpu_custom_call" | custom-call | bytes 395264 | tf_op jit(solution)/shard_map/fold/pallas_call | solution.py:594
  35.8 0.6 %collective-permute-done.12.other_ref = f32[208,128]{1,0:T(8,128)S(1)} collective-permute-done((f32[208,128]{1,0:T(8,128)S(1)}, f32[208,128]{1,0:T(8,128)S(1)}, u32[]{:S(2)}, u32[]{:S(2)}) %collective-permute-start.12) | collective-permute-done | bytes 106528 | tf_op jit(solution)/shard_map/ppermute | solution.py:802
  36.4 0.7 %finish.1 = (f32[8,128]{1,0:T(8,128)}, f32[384,128]{1,0:T(8,128)}, f32[1,128]{1,0:T(1,128)}, f32[1,8]{1,0:T(1,128)}) custom-call(f32[208,128]{1,0:T(8,128)S(1)} %gather.1.mine_ref, f32[208,128]{1,0:T(8,128)S(1)} %collective-permute-done.12.other_ref), custom_call_target="tpu_custom_call" | custom-call | bytes 414240 | tf_op jit(solution)/shard_map/finish/pallas_call | solution.py:594
  (4 shorter events, 0.1 us)
Async XLA Ops:
  1.6 5.2 %collective-permute-start = (f32[136,128]{1,0:T(8,128)S(1)}, f32[136,128]{1,0:T(8,128)S(1)}, u32[]{:S(2)}, u32[]{:S(2)}) collective-permute-start(f32[136,128]{1,0:T(8,128)S(1)} %get-tuple-element.58.refs_4_.near_ref), channel_id=1, source_target_pairs={{0,2},{2,0},{4,6},{6,4},{8,10},{10,8},{12,14},{14,12},{16,18},{18,... | collective-permute-start | bytes 208904 | tf_op jit(solution)/shard_map/ppermute | solution.py:659
  2.1 4.7 %collective-permute-start.1 = (f32[136,128]{1,0:T(8,128)S(1)}, f32[136,128]{1,0:T(8,128)S(1)}, u32[]{:S(2)}, u32[]{:S(2)}) collective-permute-start(f32[136,128]{1,0:T(8,128)S(1)} %get-tuple-element.59.refs_5_.far_ref), channel_id=1, source_target_pairs={{2,4},{4,2},{6,8},{8,6},{10,12},{12,10},{14,16},{16,14},{18,20},{2... | collective-permute-start | bytes 208904 | tf_op jit(solution)/shard_map/ppermute | solution.py:658
  9.8 5.5 %collective-permute-start.2 = (f32[192,128]{1,0:T(8,128)S(1)}, f32[192,128]{1,0:T(8,128)S(1)}, u32[]{:S(2)}, u32[]{:S(2)}) collective-permute-start(f32[192,128]{1,0:T(8,128)S(1)} %get-tuple-element.69), channel_id=1, source_target_pairs={{0,2},{2,0},{4,6},{6,4},{8,10},{10,8},{12,14},{14,12},{16,18},{18,... | collective-permute-start | bytes 294920 | tf_op jit(solution)/shard_map/ppermute | solution.py:720
  15.4 4.2 %collective-permute-start.3 = (f32[96,128]{1,0:T(8,128)S(1)}, f32[96,128]{1,0:T(8,128)S(1)}, u32[]{:S(2)}, u32[]{:S(2)}) collective-permute-start(f32[96,128]{1,0:T(8,128)S(1)} %get-tuple-element.85), channel_id=1, source_target_pairs={{0,1},{1,0},{2,6},{3,7},{4,5},{5,4},{6,2},{7,3},{8,9},{9,8},{10,14... | collective-permute-start | bytes 147464 | tf_op jit(solution)/shard_map/ppermute | solution.py:749
  17.0 2.6 %collective-permute-start.4 = (f32[128,128]{1,0:T(8,128)S(1)}, f32[128,128]{1,0:T(8,128)S(1)}, u32[]{:S(2)}, u32[]{:S(2)}) collective-permute-start(f32[128,128]{1,0:T(8,128)S(1)} %get-tuple-element.87), channel_id=1, source_target_pairs={{0,2},{2,0},{4,6},{6,4},{8,10},{10,8},{12,14},{14,12},{16,18},{18,... | collective-permute-start | bytes 196616 | tf_op jit(solution)/shard_map/ppermute | solution.py:750
  19.6 7.4 %collective-permute-start.7 = (f32[112,128]{1,0:T(8,128)S(1)}, f32[112,128]{1,0:T(8,128)S(1)}, u32[]{:S(2)}, u32[]{:S(2)}) collective-permute-start(f32[112,128]{1,0:T(8,128)S(1)} %join.1), channel_id=1, source_target_pairs={{0,20},{1,21},{2,19},{3,18},{4,16},{5,17},{6,23},{7,22},{8,28},{9,... | collective-permute-start | bytes 172040 | tf_op jit(solution)/shard_map/ppermute | solution.py:779
  23.2 5.7 %collective-permute-start.6 = (f32[112,128]{1,0:T(8,128)S(1)}, f32[112,128]{1,0:T(8,128)S(1)}, u32[]{:S(2)}, u32[]{:S(2)}) collective-permute-start(f32[112,128]{1,0:T(8,128)S(1)} %join.1), channel_id=1, source_target_pairs={{0,16},{1,17},{2,18},{3,19},{4,20},{5,21},{6,22},{7,23},{8,24},{9,... | collective-permute-start | bytes 172040 | tf_op jit(solution)/shard_map/ppermute | solution.py:779
  23.6 5.3 %collective-permute-start.5 = (f32[112,128]{1,0:T(8,128)S(1)}, f32[112,128]{1,0:T(8,128)S(1)}, u32[]{:S(2)}, u32[]{:S(2)}) collective-permute-start(f32[112,128]{1,0:T(8,128)S(1)} %join.1), channel_id=1, source_target_pairs={{0,4},{1,5},{2,3},{3,2},{4,0},{5,1},{6,7},{7,6},{8,12},{9,13},{10,... | collective-permute-start | bytes 172040 | tf_op jit(solution)/shard_map/ppermute | solution.py:779
  24.1 8.4 %collective-permute-start.8 = (f32[128,128]{1,0:T(8,128)S(1)}, f32[128,128]{1,0:T(8,128)S(1)}, u32[]{:S(2)}, u32[]{:S(2)}) collective-permute-start(f32[128,128]{1,0:T(8,128)S(1)} %get-tuple-element.91), channel_id=1, source_target_pairs={{2,4},{4,2},{6,8},{8,6},{10,12},{12,10},{14,16},{16,14},{18,20},{2... | collective-permute-start | bytes 196616 | tf_op jit(solution)/shard_map/ppermute | solution.py:781
  28.9 5.5 %collective-permute-start.11 = (f32[112,128]{1,0:T(8,128)S(1)}, f32[112,128]{1,0:T(8,128)S(1)}, u32[]{:S(2)}, u32[]{:S(2)}) collective-permute-start(f32[112,128]{1,0:T(8,128)S(1)} %add_add_fusion.mine_ref), channel_id=1, source_target_pairs={{0,9},{1,8},{2,14},{3,15},{4,13},{5,12},{6,10},{7,11},{8,1},{9,0},... | collective-permute-start | bytes 172040 | tf_op jit(solution)/shard_map/ppermute | solution.py:785
  30.3 4.4 %collective-permute-start.10 = (f32[112,128]{1,0:T(8,128)S(1)}, f32[112,128]{1,0:T(8,128)S(1)}, u32[]{:S(2)}, u32[]{:S(2)}) collective-permute-start(f32[112,128]{1,0:T(8,128)S(1)} %add_add_fusion.mine_ref), channel_id=1, source_target_pairs={{0,1},{1,0},{2,6},{3,7},{4,5},{5,4},{6,2},{7,3},{8,9},{9,8},{10,14... | collective-permute-start | bytes 172040 | tf_op jit(solution)/shard_map/ppermute | solution.py:785
  30.9 4.2 %collective-permute-start.9 = (f32[112,128]{1,0:T(8,128)S(1)}, f32[112,128]{1,0:T(8,128)S(1)}, u32[]{:S(2)}, u32[]{:S(2)}) collective-permute-start(f32[112,128]{1,0:T(8,128)S(1)} %add_add_fusion.mine_ref), channel_id=1, source_target_pairs={{0,8},{1,9},{2,10},{3,11},{4,12},{5,13},{6,14},{7,15},{8,0},{9,1},... | collective-permute-start | bytes 172040 | tf_op jit(solution)/shard_map/ppermute | solution.py:785
  35.1 1.4 %collective-permute-start.12 = (f32[208,128]{1,0:T(8,128)S(1)}, f32[208,128]{1,0:T(8,128)S(1)}, u32[]{:S(2)}, u32[]{:S(2)}) collective-permute-start(f32[208,128]{1,0:T(8,128)S(1)} %gather.1.mine_ref), channel_id=1, source_target_pairs={{0,2},{2,0},{4,6},{6,4},{8,10},{10,8},{12,14},{14,12},{16,18},{18,... | collective-permute-start | bytes 319496 | tf_op jit(solution)/shard_map/ppermute | solution.py:802
